TPU v7x, 256 devices: a whole 4x4x8 slice. The times are simulated.
256 devices in a mesh: dp: 256 (over z, y, x, core).
Axes of the slice: x: 4, y: 4, z: 8, core: 2. Of those that a mesh axis runs over, the one named last changes fastest.
Arguments:
- img_feats: bfloat16 [32768, 1536], P('dp'), may hold values from -30 to 30
- txt_feats: bfloat16 [32768, 4096], P('dp'), may hold values from -5 to 5
- img_head: bfloat16 [1536, 1024], replicated, may hold values from -0.12885337 to 0.12885337
- txt_head: bfloat16 [4096, 1024], replicated, may hold values from -0.07890625 to 0.07890625
- log_scale: float32 [1], replicated, may hold values from 3.4 to 4
- logit_bias: float32 [1], replicated, may hold values from -4 to -2
Outputs:
- loss: float32 [], replicated
- scalar_grads: float32 [2], replicated
- head_grad: float32 [1536, 1024], P('dp')
- text_grad: float32 [32768, 1024], P('dp')
All inputs are finite; a program needn't handle non-finite values.
Results may differ from a plain program's by a relative error of at most 0.001.
Values may be sent and summed in bfloat16 or wider, within the bound.
A program may use at most 128 MiB of HBM per device.

v0:
```python
import jax
import jax.numpy as jnp
from jax import lax
from jax.sharding import PartitionSpec as P

HALF = 6


EPS = 1e-06


def from_behind(array, axis, by):
    count = lax.axis_size(axis)
    return lax.ppermute(array, axis, [(i, (i + by) % count) for i in range(count)])


def normalized(feats, head):
    projected = jnp.dot(feats, head, preferred_element_type=jnp.float32)
    inv_norm = lax.rsqrt(jnp.sum(projected * projected, axis=-1, keepdims=True) + EPS)
    return (projected * inv_norm, inv_norm)


def transposed(weights, images):
    return lax.dot_general(
        weights, images, (((0,), (0,)), ((), ())), preferred_element_type=jnp.float32
    )


def tile_terms(img_low, text_block, temper, bias_v, positive):
    cosine = lax.dot_general(
        img_low, text_block, (((1,), (1,)), ((), ())), preferred_element_type=jnp.float32
    )
    logits = temper * cosine + bias_v
    target = jnp.eye(img_low.shape[0], dtype=jnp.float32) * (1.0 if positive else 0.0)
    pair_sign = 2.0 * target - 1.0
    loss_sum = -jnp.sum(jax.nn.log_sigmoid(pair_sign * logits))
    pair_grad = jax.nn.sigmoid(logits) - target
    cos_sum = jnp.sum(pair_grad * cosine)
    grad_sum = jnp.sum(pair_grad)
    weights = (temper * pair_grad).astype(jnp.bfloat16)
    img_part = jnp.dot(weights, text_block, preferred_element_type=jnp.float32)
    return ((loss_sum, cos_sum, grad_sum, img_part), weights)


def add_stats(totals, extra):
    return tuple((left + right for left, right in zip(totals, extra)))


def walk(text_block, step_by, offsets, img_low, temper, bias_v, totals, text_total):
    carried = jnp.zeros(text_total.shape, jnp.float32)
    for position, offset in enumerate(offsets):
        if position > 0:
            text_block, carried = (
                from_behind(text_block.astype(jnp.float32), "dp", step_by).astype(text_block.dtype),
                from_behind(carried, "dp", step_by),
            )
        stats, weights = tile_terms(img_low, text_block, temper, bias_v, offset == 0)
        totals = add_stats(totals, stats)
        carried = carried + transposed(weights, img_low)
    last_offset = offsets[-1]
    text_total = from_behind(carried, "dp", -last_offset)
    return (totals, text_total)


def shards(img_feats, txt_feats, img_head, txt_head, log_scale, logit_bias):
    img_unit, img_inv = normalized(img_feats, img_head)
    txt_unit, txt_inv = normalized(txt_feats, txt_head)
    img_low = img_unit.astype(jnp.bfloat16)
    txt_low = txt_unit.astype(jnp.bfloat16)
    temper = jnp.exp(log_scale[0])
    bias_v = logit_bias[0]
    zero_scalar = jnp.float32(0.0)
    totals = (zero_scalar, zero_scalar, zero_scalar, jnp.zeros(img_unit.shape, jnp.float32))
    text_total = jnp.zeros(txt_unit.shape, jnp.float32)
    start_block = from_behind(txt_low, "dp", -HALF)
    totals, text_total = walk(
        start_block, 1, list(range(-HALF, HALF + 1)), img_low, temper, bias_v, totals, text_total
    )
    loss_sum, cos_sum, grad_sum, img_dunit = totals
    text_grad = txt_inv * (
        text_total - txt_unit * jnp.sum(txt_unit * text_total, axis=-1, keepdims=True)
    )
    img_dproj = img_inv * (
        img_dunit - img_unit * jnp.sum(img_unit * img_dunit, axis=-1, keepdims=True)
    )
    img_dlow = img_dproj.astype(jnp.bfloat16)
    loss_all, cos_all, grad_all = lax.psum((loss_sum, cos_sum, grad_sum), "dp")
    pair_count = img_low.shape[0] * img_low.shape[0] * (2 * HALF + 1) * lax.axis_size("dp")
    loss = loss_all / pair_count
    scalar_grads = jnp.stack([temper * cos_all, grad_all]) / pair_count
    head_grad = (
        lax.psum_scatter(
            lax.dot_general(
                img_feats, img_dlow, (((0,), (0,)), ((), ())), preferred_element_type=jnp.float32
            ),
            "dp",
            scatter_dimension=0,
            tiled=True,
        )
        / img_low.shape[0]
    )
    return (loss, scalar_grads, head_grad, text_grad)


def solution(mesh):
    in_specs = (P("dp", None), P("dp", None), P(), P(), P(), P())
    out_specs = (P(), P(), P("dp", None), P("dp", None))
    return jax.shard_map(shards, mesh=mesh, in_specs=in_specs, out_specs=out_specs, check_vma=False)
```

profile of v0, /device:TPU:1, one launch (start us, length us, event | category | flops | bytes accessed | tf_op | source)
XLA Modules:
  0.0 457.5 jit_solution(1417465875265952287)
XLA Ops:
  7.2 5.2 %multiply_reduce_fusion.2 = (f32[128]{0:T(128)S(1)}, f32[128,1024]{1,0:T(8,128)S(1)}) fusion(bf16[128,4096]{1,0:T(8,128)(2,1)} %param.7, bf16[4096,1024]{1,0:T(8,128)(2,1)} %param.9), kind=kOutput, calls=%fused_computation.19 | convolution fusion | flops 1074003840 | bytes 9961984 | tf_op jit(solution)/shard_map/dot_general | solution.py:18
  12.5 9.9 %collective-permute-start = (bf16[128,1024]{1,0:T(8,128)(2,1)S(1)}, bf16[128,1024]{1,0:T(8,128)(2,1)S(1)}, u32[]{:S(2)}, u32[]{:S(2)}) collective-permute-start(bf16[128,1024]{1,0:T(8,128)(2,1)S(1)} %multiply_convert_fusion.1), channel_id=1, source_target_pairs={{0,250},{1,251},{2,252},{3,253},{4,254},{5,255},{6,0},{7,1},{8,2},... | collective-permute-start | bytes 786440 | tf_op jit(solution)/shard_map/ppermute | solution.py:14
  24.5 2.8 collective-permute-done
  27.4 2.6 collective-permute-start.1
  39.2 2.6 collective-permute-start.14
  45.7 6.7 %collective-permute-done.3 = bf16[128,1024]{1,0:T(8,128)(2,1)S(1)} collective-permute-done((bf16[128,1024]{1,0:T(8,128)(2,1)S(1)}, bf16[128,1024]{1,0:T(8,128)(2,1)S(1)}, u32[]{:S(2)}, u32[]{:S(2)}) %collective-permute-start.3) | collective-permute-done | bytes 262176 | tf_op jit(solution)/shard_map/ppermute | solution.py:14
  54.8 9.2 %collective-permute-done.4 = bf16[128,1024]{1,0:T(8,128)(2,1)S(1)} collective-permute-done((bf16[128,1024]{1,0:T(8,128)(2,1)S(1)}, bf16[128,1024]{1,0:T(8,128)(2,1)S(1)}, u32[]{:S(2)}, u32[]{:S(2)}) %collective-permute-start.4) | collective-permute-done | bytes 262176 | tf_op jit(solution)/shard_map/ppermute | solution.py:14
  65.5 9.8 %collective-permute-done.5 = bf16[128,1024]{1,0:T(8,128)(2,1)S(1)} collective-permute-done((bf16[128,1024]{1,0:T(8,128)(2,1)S(1)}, bf16[128,1024]{1,0:T(8,128)(2,1)S(1)}, u32[]{:S(2)}, u32[]{:S(2)}) %collective-permute-start.5) | collective-permute-done | bytes 262176 | tf_op jit(solution)/shard_map/ppermute | solution.py:14
  77.0 9.5 %collective-permute-done.6 = bf16[128,1024]{1,0:T(8,128)(2,1)S(1)} collective-permute-done((bf16[128,1024]{1,0:T(8,128)(2,1)S(1)}, bf16[128,1024]{1,0:T(8,128)(2,1)S(1)}, u32[]{:S(2)}, u32[]{:S(2)}) %collective-permute-start.6) | collective-permute-done | bytes 262176 | tf_op jit(solution)/shard_map/ppermute | solution.py:14
  87.9 9.8 %collective-permute-done.7 = bf16[128,1024]{1,0:T(8,128)(2,1)S(1)} collective-permute-done((bf16[128,1024]{1,0:T(8,128)(2,1)S(1)}, bf16[128,1024]{1,0:T(8,128)(2,1)S(1)}, u32[]{:S(2)}, u32[]{:S(2)}) %collective-permute-start.7) | collective-permute-done | bytes 262176 | tf_op jit(solution)/shard_map/ppermute | solution.py:14
  98.9 10.0 %collective-permute-done.8 = bf16[128,1024]{1,0:T(8,128)(2,1)S(1)} collective-permute-done((bf16[128,1024]{1,0:T(8,128)(2,1)S(1)}, bf16[128,1024]{1,0:T(8,128)(2,1)S(1)}, u32[]{:S(2)}, u32[]{:S(2)}) %collective-permute-start.8) | collective-permute-done | bytes 262176 | tf_op jit(solution)/shard_map/ppermute | solution.py:14
  110.3 9.9 %collective-permute-done.9 = bf16[128,1024]{1,0:T(8,128)(2,1)S(1)} collective-permute-done((bf16[128,1024]{1,0:T(8,128)(2,1)S(1)}, bf16[128,1024]{1,0:T(8,128)(2,1)S(1)}, u32[]{:S(2)}, u32[]{:S(2)}) %collective-permute-start.9) | collective-permute-done | bytes 262176 | tf_op jit(solution)/shard_map/ppermute | solution.py:14
  121.7 9.7 %collective-permute-done.10 = bf16[128,1024]{1,0:T(8,128)(2,1)S(1)} collective-permute-done((bf16[128,1024]{1,0:T(8,128)(2,1)S(1)}, bf16[128,1024]{1,0:T(8,128)(2,1)S(1)}, u32[]{:S(2)}, u32[]{:S(2)}) %collective-permute-start.10) | collective-permute-done | bytes 262176 | tf_op jit(solution)/shard_map/ppermute | solution.py:14
  132.7 9.9 %collective-permute-done.11 = bf16[128,1024]{1,0:T(8,128)(2,1)S(1)} collective-permute-done((bf16[128,1024]{1,0:T(8,128)(2,1)S(1)}, bf16[128,1024]{1,0:T(8,128)(2,1)S(1)}, u32[]{:S(2)}, u32[]{:S(2)}) %collective-permute-start.11) | collective-permute-done | bytes 262176 | tf_op jit(solution)/shard_map/ppermute | solution.py:14
  143.8 10.0 %collective-permute-done.12 = bf16[128,1024]{1,0:T(8,128)(2,1)S(1)} collective-permute-done((bf16[128,1024]{1,0:T(8,128)(2,1)S(1)}, bf16[128,1024]{1,0:T(8,128)(2,1)S(1)}, u32[]{:S(2)}, u32[]{:S(2)}) %collective-permute-start.12) | collective-permute-done | bytes 262176 | tf_op jit(solution)/shard_map/ppermute | solution.py:14
  156.9 3.8 convolution_bitcast_fusion
  160.9 7.9 %collective-permute-done.19 = f32[128,1024]{1,0:T(8,128)} collective-permute-done((f32[128,1024]{1,0:T(8,128)}, f32[128,1024]{1,0:T(8,128)}, u32[]{:S(2)}, u32[]{:S(2)}) %collective-permute-start.19) | collective-permute-done | bytes 524320 | tf_op jit(solution)/shard_map/ppermute | solution.py:14
  170.3 13.7 %collective-permute-done.20 = f32[128,1024]{1,0:T(8,128)S(1)} collective-permute-done((f32[128,1024]{1,0:T(8,128)S(1)}, f32[128,1024]{1,0:T(8,128)S(1)}, u32[]{:S(2)}, u32[]{:S(2)}) %collective-permute-start.20) | collective-permute-done | bytes 524320 | tf_op jit(solution)/shard_map/ppermute | solution.py:14
  185.5 15.1 %collective-permute-done.21 = f32[128,1024]{1,0:T(8,128)S(1)} collective-permute-done((f32[128,1024]{1,0:T(8,128)S(1)}, f32[128,1024]{1,0:T(8,128)S(1)}, u32[]{:S(2)}, u32[]{:S(2)}) %collective-permute-start.21) | collective-permute-done | bytes 524320 | tf_op jit(solution)/shard_map/ppermute | solution.py:14
  201.0 16.2 %collective-permute-done.22 = f32[128,1024]{1,0:T(8,128)S(1)} collective-permute-done((f32[128,1024]{1,0:T(8,128)S(1)}, f32[128,1024]{1,0:T(8,128)S(1)}, u32[]{:S(2)}, u32[]{:S(2)}) %collective-permute-start.22) | collective-permute-done | bytes 524320 | tf_op jit(solution)/shard_map/ppermute | solution.py:14
  217.6 16.3 %collective-permute-done.23 = f32[128,1024]{1,0:T(8,128)S(1)} collective-permute-done((f32[128,1024]{1,0:T(8,128)S(1)}, f32[128,1024]{1,0:T(8,128)S(1)}, u32[]{:S(2)}, u32[]{:S(2)}) %collective-permute-start.23) | collective-permute-done | bytes 524320 | tf_op jit(solution)/shard_map/ppermute | solution.py:14
  234.3 13.9 %collective-permute-done.24 = f32[128,1024]{1,0:T(8,128)S(1)} collective-permute-done((f32[128,1024]{1,0:T(8,128)S(1)}, f32[128,1024]{1,0:T(8,128)S(1)}, u32[]{:S(2)}, u32[]{:S(2)}) %collective-permute-start.24) | collective-permute-done | bytes 524320 | tf_op jit(solution)/shard_map/ppermute | solution.py:14
  273.8 87.8 %all-reduce.1 = (f32[]{:T(128)}, f32[1]{0:T(128)}, f32[]{:T(128)}) all-reduce(f32[]{:T(128)S(6)} %add.381, f32[1]{0:T(128)} %bitcast.3, f32[]{:T(128)S(6)} %add.406), channel_id=1, replica_groups=mesh['dp'=256] {'dp'}, use_global_device_ids=true, to_apply=%region_15.16 | all-reduce | flops 3 | bytes 24 | tf_op jit(solution)/shard_map/psum | solution.py:87
  364.2 77.7 %all-reduce.4.cloned.1.call-done = f32[1536,1024]{0,1:T(8,128)} async-done(((f32[1536,1024]{0,1:T(8,128)}), f32[1536,1024]{0,1:T(8,128)}) %all-reduce.4.cloned.1.call-update) | async-done | bytes 6291472
  (116 shorter events, 44.6 us)
Async XLA Ops:
  7.2 434.7 %all-reduce.4.cloned.1.call-start = ((), (), s32[]{:S(2)}) async-start(), calls=%async_computation | async-start | bytes 12582912
  12.5 14.8 %collective-permute-start = (bf16[128,1024]{1,0:T(8,128)(2,1)S(1)}, bf16[128,1024]{1,0:T(8,128)(2,1)S(1)}, u32[]{:S(2)}, u32[]{:S(2)}) collective-permute-start(bf16[128,1024]{1,0:T(8,128)(2,1)S(1)} %multiply_convert_fusion.1), channel_id=1, source_target_pairs={{0,250},{1,251},{2,252},{3,253},{4,254},{5,255},{6,0},{7,1},{8,2},... | collective-permute-start | bytes 786440 | tf_op jit(solution)/shard_map/ppermute | solution.py:14
  39.2 15.4 %collective-permute-start.14 = (f32[128,1024]{1,0:T(8,128)S(1)}, f32[128,1024]{1,0:T(8,128)S(1)}, u32[]{:S(2)}, u32[]{:S(2)}) collective-permute-start(f32[128,1024]{1,0:T(8,128)S(1)} %convolution_add_fusion), channel_id=1, source_target_pairs={{0,1},{1,2},{2,3},{3,4},{4,5},{5,6},{6,7},{7,8},{8,9},{9,10},{10,1... | collective-permute-start | bytes 1572872 | tf_op jit(solution)/shard_map/ppermute | solution.py:14
  41.8 10.6 %collective-permute-start.3 = (bf16[128,1024]{1,0:T(8,128)(2,1)S(1)}, bf16[128,1024]{1,0:T(8,128)(2,1)S(1)}, u32[]{:S(2)}, u32[]{:S(2)}) collective-permute-start(bf16[128,1024]{1,0:T(8,128)(2,1)S(1)} %collective-permute-done.2), channel_id=1, source_target_pairs={{0,1},{1,2},{2,3},{3,4},{4,5},{5,6},{6,7},{7,8},{8,9},{9,10},{10,1... | collective-permute-start | bytes 786440 | tf_op jit(solution)/shard_map/ppermute | solution.py:14
  52.4 11.6 %collective-permute-start.4 = (bf16[128,1024]{1,0:T(8,128)(2,1)S(1)}, bf16[128,1024]{1,0:T(8,128)(2,1)S(1)}, u32[]{:S(2)}, u32[]{:S(2)}) collective-permute-start(bf16[128,1024]{1,0:T(8,128)(2,1)S(1)} %collective-permute-done.3), channel_id=1, source_target_pairs={{0,1},{1,2},{2,3},{3,4},{4,5},{5,6},{6,7},{7,8},{8,9},{9,10},{10,1... | collective-permute-start | bytes 786440 | tf_op jit(solution)/shard_map/ppermute | solution.py:14
  54.7 21.9 %collective-permute-start.15 = (f32[128,1024]{1,0:T(8,128)S(1)}, f32[128,1024]{1,0:T(8,128)S(1)}, u32[]{:S(2)}, u32[]{:S(2)}) collective-permute-start(f32[128,1024]{1,0:T(8,128)S(1)} %add.432), channel_id=1, source_target_pairs={{0,1},{1,2},{2,3},{3,4},{4,5},{5,6},{6,7},{7,8},{8,9},{9,10},{10,1... | collective-permute-start | bytes 1572872 | tf_op jit(solution)/shard_map/ppermute | solution.py:14
  64.0 11.2 %collective-permute-start.5 = (bf16[128,1024]{1,0:T(8,128)(2,1)S(1)}, bf16[128,1024]{1,0:T(8,128)(2,1)S(1)}, u32[]{:S(2)}, u32[]{:S(2)}) collective-permute-start(bf16[128,1024]{1,0:T(8,128)(2,1)S(1)} %collective-permute-done.4), channel_id=1, source_target_pairs={{0,1},{1,2},{2,3},{3,4},{4,5},{5,6},{6,7},{7,8},{8,9},{9,10},{10,1... | collective-permute-start | bytes 786440 | tf_op jit(solution)/shard_map/ppermute | solution.py:14
  75.2 11.2 %collective-permute-start.6 = (bf16[128,1024]{1,0:T(8,128)(2,1)S(1)}, bf16[128,1024]{1,0:T(8,128)(2,1)S(1)}, u32[]{:S(2)}, u32[]{:S(2)}) collective-permute-start(bf16[128,1024]{1,0:T(8,128)(2,1)S(1)} %collective-permute-done.5), channel_id=1, source_target_pairs={{0,1},{1,2},{2,3},{3,4},{4,5},{5,6},{6,7},{7,8},{8,9},{9,10},{10,1... | collective-permute-start | bytes 786440 | tf_op jit(solution)/shard_map/ppermute | solution.py:14
  76.7 33.4 %collective-permute-start.16 = (f32[128,1024]{1,0:T(8,128)S(1)}, f32[128,1024]{1,0:T(8,128)S(1)}, u32[]{:S(2)}, u32[]{:S(2)}) collective-permute-start(f32[128,1024]{1,0:T(8,128)S(1)} %add.433), channel_id=1, source_target_pairs={{0,1},{1,2},{2,3},{3,4},{4,5},{5,6},{6,7},{7,8},{8,9},{9,10},{10,1... | collective-permute-start | bytes 1572872 | tf_op jit(solution)/shard_map/ppermute | solution.py:14
  86.5 11.2 %collective-permute-start.7 = (bf16[128,1024]{1,0:T(8,128)(2,1)S(1)}, bf16[128,1024]{1,0:T(8,128)(2,1)S(1)}, u32[]{:S(2)}, u32[]{:S(2)}) collective-permute-start(bf16[128,1024]{1,0:T(8,128)(2,1)S(1)} %collective-permute-done.6), channel_id=1, source_target_pairs={{0,1},{1,2},{2,3},{3,4},{4,5},{5,6},{6,7},{7,8},{8,9},{9,10},{10,1... | collective-permute-start | bytes 786440 | tf_op jit(solution)/shard_map/ppermute | solution.py:14
  97.7 11.2 %collective-permute-start.8 = (bf16[128,1024]{1,0:T(8,128)(2,1)S(1)}, bf16[128,1024]{1,0:T(8,128)(2,1)S(1)}, u32[]{:S(2)}, u32[]{:S(2)}) collective-permute-start(bf16[128,1024]{1,0:T(8,128)(2,1)S(1)} %collective-permute-done.7), channel_id=1, source_target_pairs={{0,1},{1,2},{2,3},{3,4},{4,5},{5,6},{6,7},{7,8},{8,9},{9,10},{10,1... | collective-permute-start | bytes 786440 | tf_op jit(solution)/shard_map/ppermute | solution.py:14
  108.9 11.2 %collective-permute-start.9 = (bf16[128,1024]{1,0:T(8,128)(2,1)S(1)}, bf16[128,1024]{1,0:T(8,128)(2,1)S(1)}, u32[]{:S(2)}, u32[]{:S(2)}) collective-permute-start(bf16[128,1024]{1,0:T(8,128)(2,1)S(1)} %collective-permute-done.8), channel_id=1, source_target_pairs={{0,1},{1,2},{2,3},{3,4},{4,5},{5,6},{6,7},{7,8},{8,9},{9,10},{10,1... | collective-permute-start | bytes 786440 | tf_op jit(solution)/shard_map/ppermute | solution.py:14
  110.2 22.4 %collective-permute-start.17 = (f32[128,1024]{1,0:T(8,128)S(1)}, f32[128,1024]{1,0:T(8,128)S(1)}, u32[]{:S(2)}, u32[]{:S(2)}) collective-permute-start(f32[128,1024]{1,0:T(8,128)S(1)} %add.434), channel_id=1, source_target_pairs={{0,1},{1,2},{2,3},{3,4},{4,5},{5,6},{6,7},{7,8},{8,9},{9,10},{10,1... | collective-permute-start | bytes 1572872 | tf_op jit(solution)/shard_map/ppermute | solution.py:14
  120.1 11.2 %collective-permute-start.10 = (bf16[128,1024]{1,0:T(8,128)(2,1)S(1)}, bf16[128,1024]{1,0:T(8,128)(2,1)S(1)}, u32[]{:S(2)}, u32[]{:S(2)}) collective-permute-start(bf16[128,1024]{1,0:T(8,128)(2,1)S(1)} %collective-permute-done.9), channel_id=1, source_target_pairs={{0,1},{1,2},{2,3},{3,4},{4,5},{5,6},{6,7},{7,8},{8,9},{9,10},{10,1... | collective-permute-start | bytes 786440 | tf_op jit(solution)/shard_map/ppermute | solution.py:14
  131.4 11.2 %collective-permute-start.11 = (bf16[128,1024]{1,0:T(8,128)(2,1)S(1)}, bf16[128,1024]{1,0:T(8,128)(2,1)S(1)}, u32[]{:S(2)}, u32[]{:S(2)}) collective-permute-start(bf16[128,1024]{1,0:T(8,128)(2,1)S(1)} %collective-permute-done.10), channel_id=1, source_target_pairs={{0,1},{1,2},{2,3},{3,4},{4,5},{5,6},{6,7},{7,8},{8,9},{9,10},{10,1... | collective-permute-start | bytes 786440 | tf_op jit(solution)/shard_map/ppermute | solution.py:14
  132.6 23.4 %collective-permute-start.18 = (f32[128,1024]{1,0:T(8,128)S(1)}, f32[128,1024]{1,0:T(8,128)S(1)}, u32[]{:S(2)}, u32[]{:S(2)}) collective-permute-start(f32[128,1024]{1,0:T(8,128)S(1)} %add.435), channel_id=1, source_target_pairs={{0,1},{1,2},{2,3},{3,4},{4,5},{5,6},{6,7},{7,8},{8,9},{9,10},{10,1... | collective-permute-start | bytes 1572872 | tf_op jit(solution)/shard_map/ppermute | solution.py:14
  142.6 11.2 %collective-permute-start.12 = (bf16[128,1024]{1,0:T(8,128)(2,1)S(1)}, bf16[128,1024]{1,0:T(8,128)(2,1)S(1)}, u32[]{:S(2)}, u32[]{:S(2)}) collective-permute-start(bf16[128,1024]{1,0:T(8,128)(2,1)S(1)} %collective-permute-done.11), channel_id=1, source_target_pairs={{0,1},{1,2},{2,3},{3,4},{4,5},{5,6},{6,7},{7,8},{8,9},{9,10},{10,1... | collective-permute-start | bytes 786440 | tf_op jit(solution)/shard_map/ppermute | solution.py:14
  156.9 11.9 %collective-permute-start.19 = (f32[128,1024]{1,0:T(8,128)}, f32[128,1024]{1,0:T(8,128)}, u32[]{:S(2)}, u32[]{:S(2)}) collective-permute-start(f32[128,1024]{1,0:T(8,128)} %add.436), channel_id=1, source_target_pairs={{0,1},{1,2},{2,3},{3,4},{4,5},{5,6},{6,7},{7,8},{8,9},{9,10},{10,1... | collective-permute-start | bytes 1572872 | tf_op jit(solution)/shard_map/ppermute | solution.py:14
  169.9 14.1 %collective-permute-start.20 = (f32[128,1024]{1,0:T(8,128)S(1)}, f32[128,1024]{1,0:T(8,128)S(1)}, u32[]{:S(2)}, u32[]{:S(2)}) collective-permute-start(f32[128,1024]{1,0:T(8,128)S(1)} %add.437), channel_id=1, source_target_pairs={{0,1},{1,2},{2,3},{3,4},{4,5},{5,6},{6,7},{7,8},{8,9},{9,10},{10,1... | collective-permute-start | bytes 1572872 | tf_op jit(solution)/shard_map/ppermute | solution.py:14
  184.1 16.5 %collective-permute-start.21 = (f32[128,1024]{1,0:T(8,128)S(1)}, f32[128,1024]{1,0:T(8,128)S(1)}, u32[]{:S(2)}, u32[]{:S(2)}) collective-permute-start(f32[128,1024]{1,0:T(8,128)S(1)} %add.438), channel_id=1, source_target_pairs={{0,1},{1,2},{2,3},{3,4},{4,5},{5,6},{6,7},{7,8},{8,9},{9,10},{10,1... | collective-permute-start | bytes 1572872 | tf_op jit(solution)/shard_map/ppermute | solution.py:14
  200.6 16.5 %collective-permute-start.22 = (f32[128,1024]{1,0:T(8,128)S(1)}, f32[128,1024]{1,0:T(8,128)S(1)}, u32[]{:S(2)}, u32[]{:S(2)}) collective-permute-start(f32[128,1024]{1,0:T(8,128)S(1)} %add.439), channel_id=1, source_target_pairs={{0,1},{1,2},{2,3},{3,4},{4,5},{5,6},{6,7},{7,8},{8,9},{9,10},{10,1... | collective-permute-start | bytes 1572872 | tf_op jit(solution)/shard_map/ppermute | solution.py:14
  217.2 16.7 %collective-permute-start.23 = (f32[128,1024]{1,0:T(8,128)S(1)}, f32[128,1024]{1,0:T(8,128)S(1)}, u32[]{:S(2)}, u32[]{:S(2)}) collective-permute-start(f32[128,1024]{1,0:T(8,128)S(1)} %add.440), channel_id=1, source_target_pairs={{0,1},{1,2},{2,3},{3,4},{4,5},{5,6},{6,7},{7,8},{8,9},{9,10},{10,1... | collective-permute-start | bytes 1572872 | tf_op jit(solution)/shard_map/ppermute | solution.py:14
  234.0 14.2 %collective-permute-start.24 = (f32[128,1024]{1,0:T(8,128)S(1)}, f32[128,1024]{1,0:T(8,128)S(1)}, u32[]{:S(2)}, u32[]{:S(2)}) collective-permute-start(f32[128,1024]{1,0:T(8,128)S(1)} %add.441), channel_id=1, source_target_pairs={{0,1},{1,2},{2,3},{3,4},{4,5},{5,6},{6,7},{7,8},{8,9},{9,10},{10,1... | collective-permute-start | bytes 1572872 | tf_op jit(solution)/shard_map/ppermute | solution.py:14
  249.0 196.9 %collective-permute-start.25 = (f32[128,1024]{1,0:T(8,128)}, f32[128,1024]{1,0:T(8,128)}, u32[]{:S(2)}, u32[]{:S(2)}) collective-permute-start(f32[128,1024]{1,0:T(8,128)} %add.442), channel_id=1, source_target_pairs={{0,250},{1,251},{2,252},{3,253},{4,254},{5,255},{6,0},{7,1},{8,2},... | collective-permute-start | bytes 1572872 | tf_op jit(solution)/shard_map/ppermute | solution.py:14
  (14 other events, 304.5 us)
Sparse Core Ops, SparseCore 0:
  160.8 281.0 all-reduce.3
where the time goes:
time: 459 us; the launch traced here: 457 us
  waiting for transfers between devices  262 us (57%)
  blocking collectives  87.8 us (19%)
  between operations  43.1 us (9%)
  matrix products  29.3 us (6%)
  starting transfers between devices  22.1 us (5%)
  other arithmetic  10.5 us (2%)
    ppermute x26, waiting for transfers between devices, from_behind(): lax.ppermute(array, axis, [(i, (i + by) % count) for i in range(count)])  184 us
    psum x1, blocking collectives, shards(): loss_all, cos_all, grad_all = lax.psum((loss_sum, cos_sum, grad_sum), 'dp')  87.8 us
    unnamed x2, waiting for transfers between devices  77.7 us
    ppermute x26, starting transfers between devices, from_behind(): lax.ppermute(array, axis, [(i, (i + by) % count) for i in range(count)])  22 us
    dot_general x13, matrix products, tile_terms(): lax.dot_general(img_low, text_block, (((1,), (1,)), ((), ())), preferred_...  12.3 us
  transfers between devices with their start and end apart: 27, of which 20 were waited for; matrix products, arithmetic and copies ran while one was open for 7% of the time, Pallas kernels for 0%

commit v1 on v0

v1 whole, which is shorter than its diff:
```python
import jax
import jax.numpy as jnp
from jax import lax
from jax.experimental import pallas as pl
from jax.experimental.pallas import tpu as pltpu
from jax.sharding import PartitionSpec as P

EPS = 1e-06
B = 128
E = 1024
DI = 1536
DT = 4096
N = 256
PAIRS = 54525952
CH = 512

TXT = 0
IMG = 24
FEA = 48
DLO = 52
SIB = 56
PLN = 58
OWN = 74
IDS = 82


def kernel(
    ls_ref, lb_ref, imgf_ref, txtf_ref, imgh_ref, txth_ref,
    st_ref, hg_ref, tg_ref, tinv_ref,
    txtf, imgh, txth, feats, texts, images, unit_t, unit_i, acc_t, acc_i, inv_t, inv_i,
    dlow_t, dgat, stat, stats2, tails, part_sib, part_rcv, part, plane, owned, pieces,
    load_sem, send_sem, recv_sem,
):
    me = lax.axis_index("dp")
    core = lax.rem(me, 2)
    spot = lax.rem(me // 2, 16)
    z = me // 32
    x = lax.rem(spot, 4)
    row_first = me - 2 * x
    right_x = lax.rem(x + 1, 4)
    left_x = lax.rem(x + 3, 4)
    right = row_first + 2 * right_x
    left = row_first + 2 * left_x
    inner = (x == 1) | (x == 2)
    up = lax.rem(me + 8, N)
    down = lax.rem(me + N - 8, N)
    sib = me + 1 - 2 * core

    side = 1 - 2 * core

    def z_mate(off):
        return lax.rem(me + 32 * off + N, N)

    def quarter(off):
        return lax.rem(z + off + 8, 4)

    def plane_mate(off):
        return 32 * z + 2 * lax.rem(spot + off, 16) + core

    first_owner = 128 * core + 8 * spot
    my_row = me // 8
    src_core = my_row // 16
    src_spot = lax.rem(my_row, 16)

    def source(zz):
        return 32 * zz + 2 * src_spot + src_core

    barrier = pltpu.get_barrier_semaphore()

    def greet(dev):
        pl.semaphore_signal(barrier, inc=1, device_id={"dp": dev}, device_id_type=pl.DeviceIdType.MESH)

    for dev in [right, left, up, down, sib] + [z_mate(side), z_mate(2 * side), z_mate(-side)] + [plane_mate(o) for o in range(1, 16)]:
        greet(dev)
    for zz in range(8):
        @pl.when(source(zz) != me)
        def _():
            greet(source(zz))

    loads = {}

    def load(i, src, dst):
        loads[i] = pltpu.make_async_copy(src, dst, load_sem.at[i])
        loads[i].start()

    load(0, imgf_ref, feats.at[pl.ds(0, B)])
    load(1, txtf_ref, txtf)
    for j in range(DT // CH):
        load(2 + j, txth_ref.at[pl.ds(j * CH, CH)], txth.at[pl.ds(j * CH, CH)])
    for j in range(DI // CH):
        load(10 + j, imgh_ref.at[pl.ds(j * CH, CH)], imgh.at[pl.ds(j * CH, CH)])

    owner_is_me = (me >= first_owner) & (me < first_owner + 8)
    pl.semaphore_wait(barrier, 23 + 8 - owner_is_me.astype(jnp.int32))

    sent = []
    sent_if = []

    def copy(i, src, dst, dev):
        return pltpu.make_async_remote_copy(
            src_ref=src, dst_ref=dst, send_sem=send_sem.at[i], recv_sem=recv_sem.at[i],
            device_id={"dp": dev}, device_id_type=pl.DeviceIdType.MESH,
        )

    def send(i, src, dst, dev):
        c = copy(i, src, dst, dev)
        c.start()
        sent.append(c)

    def send_if(cond, i, src, dst, dev, landing=None):
        c = pltpu.make_async_remote_copy(
            src_ref=src, dst_ref=dst, send_sem=send_sem.at[i],
            recv_sem=recv_sem.at[i if landing is None else landing],
            device_id={"dp": dev}, device_id_type=pl.DeviceIdType.MESH,
        )

        @pl.when(cond)
        def _():
            c.start()

        sent_if.append((cond, c))

    def arrived(i, dst):
        copy(i, dst, dst, sib).wait_recv()

    def fea(n):
        return feats.at[pl.ds(n * B, B)]

    def in_row(at, q):
        return q - 4 * (at + q >= 4).astype(jnp.int32)

    def crossed(at, q):
        return q - 4 * (at + q < 4).astype(jnp.int32)

    def slot(ref, off, half=None):
        if half is None:
            return ref.at[2 * (3 + off) + core]
        return ref.at[2 * (3 + off) + core, pl.ds(half * (B // 2), B // 2)]

    def row_send(base, ref, half):
        send(base + 4 + (half or 0), slot(ref, 0, half), slot(ref, in_row(right_x, 3), half), right)
        send(base + (half or 0), slot(ref, 0, half), slot(ref, in_row(left_x, 1), half), left)

    def row_wait(base, ref, q, half):
        arrived(base + 2 * (q - 1) + (half or 0), slot(ref, in_row(x, q), half))

    def opposite_send(base, ref, half):
        at = lax.rem(x + side + 4, 4)
        send(
            base + 2 + (half or 0), slot(ref, in_row(x, 2 + side), half), slot(ref, in_row(at, 2), half),
            row_first + 2 * at,
        )

    def cross_send(base, ref, q, half):
        dev = jnp.where(x + q < 4, up, down)
        i = base + 6 + 2 * (q - 1) + (half or 0)
        src, dst = slot(ref, in_row(x, q), half), slot(ref, crossed(x, q), half)
        if q == 2:
            send_if(inner, i, src, dst, dev)
        else:
            send(i, src, dst, dev)

    def cross_wait(base, ref, q, half):
        arrived(base + 6 + 2 * (q - 1) + (half or 0), slot(ref, crossed(x, q), half))

    def cross_wait_rest(base, ref, q, half):
        @pl.when(x != (q + 1) // 2)
        def _():
            cross_wait(base, ref, q, half)

    def hand_on(base, ref, half):
        for at in (1, 2):
            @pl.when(x == at)
            def _():
                cross_wait(base, ref, 2 * at - 1, half)
        near = jnp.where(inner, x, 1)
        taken = crossed(near, 2 * near - 1)
        to = 3 * (near - 1)
        send_if(
            inner, base + 12 + (half or 0), slot(ref, taken, half), slot(ref, crossed(to, 2), half),
            row_first + 2 * to, base + 8 + (half or 0),
        )

    def sib_send(base, ref, n, off):
        send(base + 14 + n, slot(ref, off), slot(ref, off), sib)

    def sib_wait(base, ref, n, off):
        arrived(base + 14 + n, ref.at[2 * (3 + off) + 1 - core])

    def project(read, head, acc, first, count):
        acc[...] = jnp.zeros((B, E), jnp.float32)
        for j in range(count):
            loads[first + j].wait()
            acc[...] += jnp.dot(read(j), head[pl.ds(j * CH, CH), :], preferred_element_type=jnp.float32)

    def normalize(acc, unit, inv, ref):
        proj = acc[...]
        scale = lax.rsqrt(jnp.sum(proj * proj, axis=-1, keepdims=True) + EPS)
        value = proj * scale
        unit[...] = value
        inv[...] = jnp.broadcast_to(scale, (B, 128))
        ref[6 + core] = value.astype(jnp.bfloat16)

    loads[0].wait()
    send(FEA + 1, fea(0), fea(1), z_mate(-side))
    send(FEA + 3, fea(0), fea(3), z_mate(side))
    loads[1].wait()
    project(lambda j: txtf[:, pl.ds(j * CH, CH)], txth, acc_t, 2, DT // CH)
    normalize(acc_t, unit_t, inv_t, texts)
    for half in (0, 1):
        row_send(TXT, texts, half)
    sib_send(TXT, texts, 0, 0)
    project(lambda j: feats[pl.ds(0, B), pl.ds(j * CH, CH)], imgh, acc_i, 10, DI // CH)
    normalize(acc_i, unit_i, inv_i, images)
    sib_send(IMG, images, 0, 0)

    temper = jnp.exp(jnp.full((1, 2 * B), ls_ref[0], jnp.float32))
    bias = lb_ref[0]
    rows = lax.broadcasted_iota(jnp.int32, (B, 2 * B), 0)
    cols = lax.broadcasted_iota(jnp.int32, (B, 2 * B), 1)
    acc_i[...] = jnp.zeros((B, E), jnp.float32)
    acc_t[...] = jnp.zeros((B, E), jnp.float32)
    totals = [jnp.zeros((1, 2 * B), jnp.float32) for _ in range(3)]

    def pair(base, own, ref, n, acc, stats):
        off = 0 if n == 0 else in_row(x, n) if n < 4 else crossed(x, n - 3)
        sib_wait(base, ref, n, off)
        block = ref[pl.ds(2 * (3 + off), 2)].reshape(2 * B, E)
        cosine = lax.dot_general(
            own[6 + core], block, (((1,), (1,)), ((), ())), preferred_element_type=jnp.float32
        )
        logits = temper * cosine + bias
        small = jnp.exp(-jnp.abs(logits))
        grad = jnp.where(logits >= 0.0, 1.0, small) / (1.0 + small)
        if n == 0:
            hit = cols == rows + core * B
            grad = grad - jnp.where(hit, 1.0, 0.0)
        else:
            apart = 2 * off - core + (cols >= B).astype(jnp.int32)
            valid = (apart >= -6) & (apart <= 6)
            grad = jnp.where(valid, grad, 0.0)
        if stats:
            signed = jnp.where(hit, -logits, logits) if n == 0 else logits
            loss = jnp.maximum(signed, 0.0) + jnp.log1p(small)
            if n > 0:
                loss = jnp.where(valid, loss, 0.0)
            for k, term in enumerate((loss, grad * cosine, grad)):
                totals[k] = totals[k] + jnp.sum(term, axis=0, keepdims=True)
        weights = (temper * grad).astype(jnp.bfloat16)
        acc[...] += jnp.dot(weights, block, preferred_element_type=jnp.float32)

    def text_pair(n):
        pair(TXT, images, texts, n, acc_i, True)

    def image_pair(n):
        pair(IMG, texts, images, n, acc_t, False)

    text_pair(0)
    for half in (0, 1):
        for q in (1, 3):
            row_wait(TXT, texts, q, half)
            cross_send(TXT, texts, q, half)
        opposite_send(TXT, texts, half)
    for q in (1, 3):
        sib_send(TXT, texts, q, in_row(x, q))
    arrived(FEA + 1, fea(1))
    send(FEA + 2, fea(1), fea(2), z_mate(-side))
    text_pair(1)
    for half in (0, 1):
        row_wait(TXT, texts, 2, half)
        cross_send(TXT, texts, 2, half)
        hand_on(TXT, texts, half)
    sib_send(TXT, texts, 2, in_row(x, 2))
    text_pair(3)
    row_send(IMG, images, None)
    text_pair(2)
    for q in (1, 3):
        for half in (0, 1):
            cross_wait_rest(TXT, texts, q, half)
        sib_send(TXT, texts, 3 + q, crossed(x, q))
    text_pair(4)
    text_pair(6)
    for half in (0, 1):
        cross_wait(TXT, texts, 2, half)
    sib_send(TXT, texts, 5, crossed(x, 2))
    text_pair(5)

    stat[...] = jnp.zeros((8, 2 * B), jnp.float32)
    stat[0:1, 0:B] = totals[0][:, :B] + totals[0][:, B:]
    stat[0:1, B : 2 * B] = totals[1][:, :B] + totals[1][:, B:]
    stat[1:2, 0:B] = totals[2][:, :B] + totals[2][:, B:]
    send(SIB + 1, stat, stats2, sib)
    unit = unit_i[...]
    dunit = acc_i[...]
    dproj = inv_i[:, 0:1] * (dunit - unit * jnp.sum(unit * dunit, axis=-1, keepdims=True))
    for j in range(4):
        dlow_t[j] = dproj[:, j * 256 : (j + 1) * 256].T.astype(jnp.bfloat16)

    def window(n):
        return dgat.at[:, pl.ds(n * B, B)]

    for n, off in ((1, -side), (2, -2 * side), (3, side)):
        send(DLO + n, dlow_t.at[quarter(off)], window(n), z_mate(off))
    dgat[:, 0:B] = dlow_t[quarter(0)]
    for q in (1, 3):
        row_wait(IMG, images, q, None)
        cross_send(IMG, images, q, None)
    opposite_send(IMG, images, None)
    for q in (1, 3):
        sib_send(IMG, images, q, in_row(x, q))
    for n in (0, 1, 3):
        image_pair(n)

    for n in (1, 2, 3):
        arrived(DLO + n, window(n))
    arrived(FEA + 2, fea(2))
    arrived(FEA + 3, fea(3))

    def product(half, ref):
        for n in range(3):
            res = jnp.dot(
                dgat[...], feats[:, pl.ds(pl.multiple_of(half * 768 + n * 256, 256), 256)],
                preferred_element_type=jnp.float32,
            ).T
            ref[pl.ds(n * 256, 256), :] = res

    product(1 - core, part_sib)
    send(SIB, part_sib, part_rcv, sib)
    product(core, part)
    arrived(SIB, part_rcv)
    arrived(SIB + 1, stats2)
    both = stat[...] + stats2[...]
    for t in range(16):
        pieces[t, 0:48, :] = part[t * 48 : (t + 1) * 48, :] + part_rcv[t * 48 : (t + 1) * 48, :]
        pieces[t, 48:56, :] = both
    for o in range(1, 16):
        send(PLN + o, pieces.at[lax.rem(spot + o, 16)], plane.at[spot], plane_mate(o))
    plane[spot] = pieces[spot]

    row_wait(IMG, images, 2, None)
    cross_send(IMG, images, 2, None)
    sib_send(IMG, images, 2, in_row(x, 2))
    hand_on(IMG, images, None)
    for q in (1, 3):
        cross_wait_rest(IMG, images, q, None)
        sib_send(IMG, images, 3 + q, crossed(x, q))
    image_pair(2)

    for o in range(1, 16):
        arrived(PLN + o, plane.at[lax.rem(spot + 16 - o, 16)])
    total = jnp.sum(plane[...], axis=0)
    for j in range(8):
        tails[j, 0:6, :] = total[6 * j : 6 * j + 6, :]
        tails[j, 6:8, :] = total[48:50, :]
    for j in range(8):
        @pl.when(first_owner + j != me)
        def _():
            pltpu.make_async_remote_copy(
                src_ref=tails.at[j], dst_ref=owned.at[z],
                send_sem=send_sem.at[OWN + j], recv_sem=recv_sem.at[OWN + z],
                device_id={"dp": first_owner + j}, device_id_type=pl.DeviceIdType.MESH,
            ).start()

        @pl.when(first_owner + j == me)
        def _():
            owned[z] = tails[j]

    image_pair(4)
    image_pair(6)
    cross_wait(IMG, images, 2, None)
    sib_send(IMG, images, 5, crossed(x, 2))
    image_pair(5)
    unit = unit_t[...]
    dunit = acc_t[...]
    tg_ref[...] = dunit - unit * jnp.sum(unit * dunit, axis=-1, keepdims=True)
    tinv_ref[...] = inv_t[...]

    for zz in range(8):
        @pl.when(source(zz) != me)
        def _():
            arrived(OWN + zz, owned.at[zz])
    for n in range(4):
        hg_ref[:, n * 256 : (n + 1) * 256] = owned[n, 0:6, :] + owned[n + 4, 0:6, :]
    st_ref[...] = jnp.sum(owned[...], axis=0)
    for j in range(8):
        @pl.when(first_owner + j != me)
        def _():
            copy(OWN + j, tails.at[j], owned.at[z], first_owner + j).wait_send()
    for c in sent:
        c.wait_send()
    for cond, c in sent_if:
        @pl.when(cond)
        def _():
            c.wait_send()


def finish(ls_ref, st_ref, hgs_ref, tgs_ref, tinv_ref, loss_ref, sg_ref, hg_ref, tg_ref):
    temper = jnp.exp(jnp.full((1, B), ls_ref[0], jnp.float32))
    loss_ref[0] = jnp.sum(st_ref[6:7, 0:B]) / PAIRS
    sg_ref[0] = jnp.sum(st_ref[6:7, B : 2 * B] * temper) / PAIRS
    sg_ref[1] = jnp.sum(st_ref[7:8, 0:B]) / PAIRS
    hg_ref[...] = hgs_ref[...] * (1.0 / B)
    tg_ref[...] = tgs_ref[...] * tinv_ref[:, 0:1]


def shards(img_feats, txt_feats, img_head, txt_head, log_scale, logit_bias):
    f32, bf16 = jnp.float32, jnp.bfloat16
    smem = pl.BlockSpec(memory_space=pltpu.SMEM)
    vmem = pl.BlockSpec(memory_space=pltpu.VMEM)
    hbm = pl.BlockSpec(memory_space=pl.ANY)
    sums = pl.pallas_call(
        kernel,
        out_shape=(
            jax.ShapeDtypeStruct((8, 2 * B), f32),
            jax.ShapeDtypeStruct((6, E), f32),
            jax.ShapeDtypeStruct((B, E), f32),
            jax.ShapeDtypeStruct((B, 128), f32),
        ),
        in_specs=[smem] * 2 + [hbm] * 4,
        out_specs=(vmem,) * 4,
        scratch_shapes=[
            pltpu.VMEM((B, DT), bf16),
            pltpu.VMEM((DI, E), bf16),
            pltpu.VMEM((DT, E), bf16),
            pltpu.VMEM((4 * B, DI), bf16),
            pltpu.VMEM((14, B, E), bf16),
            pltpu.VMEM((14, B, E), bf16),
            pltpu.VMEM((B, E), f32),
            pltpu.VMEM((B, E), f32),
            pltpu.VMEM((B, E), f32),
            pltpu.VMEM((B, E), f32),
            pltpu.VMEM((B, 128), f32),
            pltpu.VMEM((B, 128), f32),
            pltpu.VMEM((4, 256, B), bf16),
            pltpu.VMEM((256, 4 * B), bf16),
            pltpu.VMEM((8, 256), f32),
            pltpu.VMEM((8, 256), f32),
            pltpu.VMEM((8, 8, 256), f32),
            pltpu.VMEM((768, 256), f32),
            pltpu.VMEM((768, 256), f32),
            pltpu.VMEM((768, 256), f32),
            pltpu.VMEM((16, 56, 256), f32),
            pltpu.VMEM((8, 8, 256), f32),
            pltpu.VMEM((16, 56, 256), f32),
            pltpu.SemaphoreType.DMA((16,)),
            pltpu.SemaphoreType.DMA((IDS,)),
            pltpu.SemaphoreType.DMA((IDS,)),
        ],
        compiler_params=pltpu.CompilerParams(
            collective_id=0, has_side_effects=True, vmem_limit_bytes=62 * 2**20
        ),
        cost_estimate=pl.CostEstimate(flops=5 * 10**9, bytes_accessed=14 * 10**6, transcendentals=10**6),
        name="contrastive",
    )(log_scale, logit_bias, img_feats, txt_feats, img_head, txt_head)
    loss, scalar_grads, head_grad, text_grad = pl.pallas_call(
        finish,
        out_shape=(
            jax.ShapeDtypeStruct((1,), f32),
            jax.ShapeDtypeStruct((2,), f32),
            jax.ShapeDtypeStruct((6, E), f32),
            jax.ShapeDtypeStruct((B, E), f32),
        ),
        in_specs=[smem] + [vmem] * 4,
        out_specs=(smem, smem, vmem, vmem),
        name="finish",
    )(log_scale, *sums)
    return loss.reshape(()), scalar_grads, head_grad, text_grad


def solution(mesh):
    in_specs = (P("dp", None), P("dp", None), P(), P(), P(), P())
    out_specs = (P(), P(), P("dp", None), P("dp", None))
    return jax.shard_map(shards, mesh=mesh, in_specs=in_specs, out_specs=out_specs, check_vma=False)
```

time: 459 us -> 76.4 us (0.17)
  waiting for transfers between devices: 262 us -> 0 us
  blocking collectives: 87.8 us -> 0 us
  Pallas kernels: 0 us -> 74.3 us
  between operations: 43.1 us -> 1.93 us
  matrix products: 29.3 us -> 0 us
  starting transfers between devices: 22.1 us -> 0 us
  other arithmetic: 10.5 us -> 0 us
    ppermute x26 -> x0, waiting for transfers between devices: 184 us -> none  [from_behind(): lax.ppermute(array, axis, [(i, (i + by) % count) for i in range(count)])]
    psum x1 -> x0, blocking collectives: 87.8 us -> none  [shards(): loss_all, cos_all, grad_all = lax.psum((loss_sum, cos_sum, grad_sum), 'dp')]
    unnamed x2 -> x0, waiting for transfers between devices: 77.7 us -> none
    pallas_call x0 -> x2, Pallas kernels: none -> 74.3 us  [the longest x1 72.3 us: shards(): pl.pallas_call(kernel, out_shape=(jax.ShapeDtypeStruct((8, 2 * B), f32),...]
    dot_general x42 -> x0, matrix products: 29.3 us -> none  [the longest x13 12.3 us: tile_terms(): lax.dot_general(img_low, text_block, (((1,), (1,)), ((), ())), preferred_...]
    ppermute x26 -> x0, starting transfers between devices: 22 us -> none  [from_behind(): lax.ppermute(array, axis, [(i, (i + by) % count) for i in range(count)])]
  transfers between devices with their start and end apart: 27 -> 0, of which waited for: 20 -> 0; matrix products, arithmetic and copies ran while one was open for 7% -> 0% of each run, Pallas kernels for 0% -> 0%
where the time goes in v1:
time: 76.4 us; the launch traced here: 76.3 us
  Pallas kernels  74.3 us (97%)
  between operations  1.93 us (3%)
    pallas_call x1, Pallas kernels, shards(): pl.pallas_call(kernel, out_shape=(jax.ShapeDtypeStruct((8, 2 * B), f32),...  72.3 us
    pallas_call x1, Pallas kernels, shards(): pl.pallas_call(finish, out_shape=(jax.ShapeDtypeStruct((1,), f32), jax.Sh...  2.02 us

profile of v1, /device:TPU:1, one launch (start us, length us, event | category | flops | bytes accessed | tf_op | source)
XLA Modules:
  0.0 76.3 jit_solution(4948108422397231871)
XLA Ops:
  1.9 72.3 %contrastive.1 = (f32[8,256]{1,0:T(8,128)}, f32[6,1024]{1,0:T(8,128)}, f32[128,1024]{1,0:T(8,128)}, f32[128,128]{1,0:T(8,128)}) custom-call(f32[1]{0:T(128)S(6)} %copy.10.ls_ref, f32[1]{0:T(128)S(6)} %copy.11.lb_ref, bf16[128,1536]{1,0:T(8,128)(2,1)} %imgf_ref.1, bf16[128,4096]{1,0:T(8,128)(2,1)} %txtf_ref.1, bf16[1536,1024]{1,0:T(8,128)(2,1)} %imgh_ref.1, ...), custom_call_target="tpu_custom_call" | custom-call | flops 5000000000 | bytes 14000000 | tf_op jit(solution)/shard_map/contrastive/pallas_call | solution.py:411
  74.2 2.0 %finish.1 = (f32[1]{0:T(128)}, f32[2]{0:T(128)}, f32[6,1024]{1,0:T(8,128)}, f32[128,1024]{1,0:T(8,128)}) custom-call(f32[1]{0:T(128)S(6)} %copy.10.ls_ref, f32[8,256]{1,0:T(8,128)} %get-tuple-element.12.st_ref, f32[6,1024]{1,0:T(8,128)} %get-tuple-element.13.hgs_ref, f32[128,1024]{1,0:T(8,128)} %get-tuple-element.14.tgs_ref, ...), custom_call_target="tpu_custom_call" | custom-call | tf_op jit(solution)/shard_map/finish/pallas_call | solution.py:455

commit v2 on v1

--- a/solution.py
+++ b/solution.py
@@ -19,9 +19,9 @@
 FEA = 48
 DLO = 52
 SIB = 56
-PLN = 58
-OWN = 74
-IDS = 82
+PLN = 60
+OWN = 76
+IDS = 84
 
 
 def kernel(
@@ -91,7 +91,6 @@
         load(10 + j, imgh_ref.at[pl.ds(j * CH, CH)], imgh.at[pl.ds(j * CH, CH)])
 
     owner_is_me = (me >= first_owner) & (me < first_owner + 8)
-    pl.semaphore_wait(barrier, 23 + 8 - owner_is_me.astype(jnp.int32))
 
     sent = []
     sent_if = []
@@ -201,15 +200,16 @@
         inv[...] = jnp.broadcast_to(scale, (B, 128))
         ref[6 + core] = value.astype(jnp.bfloat16)
 
+    loads[1].wait()
+    project(lambda j: txtf[:, pl.ds(j * CH, CH)], txth, acc_t, 2, DT // CH)
+    normalize(acc_t, unit_t, inv_t, texts)
+    pl.semaphore_wait(barrier, 23 + 8 - owner_is_me.astype(jnp.int32))
+    for half in (0, 1):
+        row_send(TXT, texts, half)
+    sib_send(TXT, texts, 0, 0)
     loads[0].wait()
     send(FEA + 1, fea(0), fea(1), z_mate(-side))
     send(FEA + 3, fea(0), fea(3), z_mate(side))
-    loads[1].wait()
-    project(lambda j: txtf[:, pl.ds(j * CH, CH)], txth, acc_t, 2, DT // CH)
-    normalize(acc_t, unit_t, inv_t, texts)
-    for half in (0, 1):
-        row_send(TXT, texts, half)
-    sib_send(TXT, texts, 0, 0)
     project(lambda j: feats[pl.ds(0, B), pl.ds(j * CH, CH)], imgh, acc_i, 10, DI // CH)
     normalize(acc_i, unit_i, inv_i, images)
     sib_send(IMG, images, 0, 0)
@@ -222,40 +222,45 @@
     acc_t[...] = jnp.zeros((B, E), jnp.float32)
     totals = [jnp.zeros((1, 2 * B), jnp.float32) for _ in range(3)]
 
-    def pair(base, own, ref, n, acc, stats):
-        off = 0 if n == 0 else in_row(x, n) if n < 4 else crossed(x, n - 3)
-        sib_wait(base, ref, n, off)
-        block = ref[pl.ds(2 * (3 + off), 2)].reshape(2 * B, E)
-        cosine = lax.dot_general(
-            own[6 + core], block, (((1,), (1,)), ((), ())), preferred_element_type=jnp.float32
-        )
-        logits = temper * cosine + bias
-        small = jnp.exp(-jnp.abs(logits))
-        grad = jnp.where(logits >= 0.0, 1.0, small) / (1.0 + small)
-        if n == 0:
-            hit = cols == rows + core * B
-            grad = grad - jnp.where(hit, 1.0, 0.0)
-        else:
-            apart = 2 * off - core + (cols >= B).astype(jnp.int32)
-            valid = (apart >= -6) & (apart <= 6)
-            grad = jnp.where(valid, grad, 0.0)
-        if stats:
-            signed = jnp.where(hit, -logits, logits) if n == 0 else logits
-            loss = jnp.maximum(signed, 0.0) + jnp.log1p(small)
-            if n > 0:
-                loss = jnp.where(valid, loss, 0.0)
-            for k, term in enumerate((loss, grad * cosine, grad)):
-                totals[k] = totals[k] + jnp.sum(term, axis=0, keepdims=True)
-        weights = (temper * grad).astype(jnp.bfloat16)
-        acc[...] += jnp.dot(weights, block, preferred_element_type=jnp.float32)
-
-    def text_pair(n):
-        pair(TXT, images, texts, n, acc_i, True)
-
-    def image_pair(n):
-        pair(IMG, texts, images, n, acc_t, False)
-
-    text_pair(0)
+    def pairs(base, own, ref, numbers, acc, stats):
+        offs = [0 if n == 0 else in_row(x, n) if n < 4 else crossed(x, n - 3) for n in numbers]
+        for n, off in zip(numbers, offs):
+            sib_wait(base, ref, n, off)
+        added = None
+        for n, off in zip(numbers, offs):
+            block = ref[pl.ds(2 * (3 + off), 2)].reshape(2 * B, E)
+            cosine = lax.dot_general(
+                own[6 + core], block, (((1,), (1,)), ((), ())), preferred_element_type=jnp.float32
+            )
+            logits = temper * cosine + bias
+            small = jnp.exp(-jnp.abs(logits))
+            grad = jnp.where(logits >= 0.0, 1.0, small) / (1.0 + small)
+            if n == 0:
+                hit = cols == rows + core * B
+                grad = grad - jnp.where(hit, 1.0, 0.0)
+            else:
+                apart = 2 * off - core + (cols >= B).astype(jnp.int32)
+                valid = (apart >= -6) & (apart <= 6)
+                grad = jnp.where(valid, grad, 0.0)
+            if stats:
+                signed = jnp.where(hit, -logits, logits) if n == 0 else logits
+                loss = jnp.maximum(signed, 0.0) + jnp.log1p(small)
+                if n > 0:
+                    loss = jnp.where(valid, loss, 0.0)
+                for k, term in enumerate((loss, grad * cosine, grad)):
+                    totals[k] = totals[k] + jnp.sum(term, axis=0, keepdims=True)
+            weights = (temper * grad).astype(jnp.bfloat16)
+            term = jnp.dot(weights, block, preferred_element_type=jnp.float32)
+            added = term if added is None else added + term
+        acc[...] += added
+
+    def text_pairs(*numbers):
+        pairs(TXT, images, texts, numbers, acc_i, True)
+
+    def image_pairs(*numbers):
+        pairs(IMG, texts, images, numbers, acc_t, False)
+
+    text_pairs(0)
     for half in (0, 1):
         for q in (1, 3):
             row_wait(TXT, texts, q, half)
@@ -263,33 +268,31 @@
         opposite_send(TXT, texts, half)
     for q in (1, 3):
         sib_send(TXT, texts, q, in_row(x, q))
-    arrived(FEA + 1, fea(1))
-    send(FEA + 2, fea(1), fea(2), z_mate(-side))
-    text_pair(1)
     for half in (0, 1):
         row_wait(TXT, texts, 2, half)
         cross_send(TXT, texts, 2, half)
         hand_on(TXT, texts, half)
     sib_send(TXT, texts, 2, in_row(x, 2))
-    text_pair(3)
+    arrived(FEA + 1, fea(1))
+    send(FEA + 2, fea(1), fea(2), z_mate(-side))
+    text_pairs(1, 3)
     row_send(IMG, images, None)
-    text_pair(2)
+    text_pairs(2)
     for q in (1, 3):
         for half in (0, 1):
             cross_wait_rest(TXT, texts, q, half)
         sib_send(TXT, texts, 3 + q, crossed(x, q))
-    text_pair(4)
-    text_pair(6)
+    text_pairs(4, 6)
     for half in (0, 1):
         cross_wait(TXT, texts, 2, half)
     sib_send(TXT, texts, 5, crossed(x, 2))
-    text_pair(5)
+    text_pairs(5)
 
     stat[...] = jnp.zeros((8, 2 * B), jnp.float32)
     stat[0:1, 0:B] = totals[0][:, :B] + totals[0][:, B:]
     stat[0:1, B : 2 * B] = totals[1][:, :B] + totals[1][:, B:]
     stat[1:2, 0:B] = totals[2][:, :B] + totals[2][:, B:]
-    send(SIB + 1, stat, stats2, sib)
+    send(SIB + 2, stat, stats2, sib)
     unit = unit_i[...]
     dunit = acc_i[...]
     dproj = inv_i[:, 0:1] * (dunit - unit * jnp.sum(unit * dunit, axis=-1, keepdims=True))
@@ -308,33 +311,42 @@
     opposite_send(IMG, images, None)
     for q in (1, 3):
         sib_send(IMG, images, q, in_row(x, q))
-    for n in (0, 1, 3):
-        image_pair(n)
+    image_pairs(0)
+    image_pairs(1, 3)
 
     for n in (1, 2, 3):
         arrived(DLO + n, window(n))
     arrived(FEA + 2, fea(2))
     arrived(FEA + 3, fea(3))
 
-    def product(half, ref):
-        for n in range(3):
-            res = jnp.dot(
-                dgat[...], feats[:, pl.ds(pl.multiple_of(half * 768 + n * 256, 256), 256)],
-                preferred_element_type=jnp.float32,
-            ).T
-            ref[pl.ds(n * 256, 256), :] = res
-
-    product(1 - core, part_sib)
-    send(SIB, part_sib, part_rcv, sib)
-    product(core, part)
-    arrived(SIB, part_rcv)
-    arrived(SIB + 1, stats2)
+    def part_rows(ref, n):
+        return ref.at[pl.ds(pl.multiple_of(n * 384, 384), 384)]
+
+    def product(half, n, ref):
+        columns = pl.ds(pl.multiple_of(half * 768 + n * 384, 128), 384)
+        part_rows(ref, n)[...] = jnp.dot(
+            dgat[...], feats[:, columns], preferred_element_type=jnp.float32
+        ).T
+
+    for j, n in enumerate((1 - core, core)):
+        product(1 - core, n, part_sib)
+        send(SIB + j, part_rows(part_sib, n), part_rows(part_rcv, n), sib)
+    for n in (core, 1 - core):
+        product(core, n, part)
+    arrived(SIB + 2, stats2)
     both = stat[...] + stats2[...]
-    for t in range(16):
-        pieces[t, 0:48, :] = part[t * 48 : (t + 1) * 48, :] + part_rcv[t * 48 : (t + 1) * 48, :]
-        pieces[t, 48:56, :] = both
-    for o in range(1, 16):
-        send(PLN + o, pieces.at[lax.rem(spot + o, 16)], plane.at[spot], plane_mate(o))
+    for j, n in enumerate((core, 1 - core)):
+        arrived(SIB + j, part_rows(part_rcv, n))
+        for i in range(8):
+            span = pl.ds(pl.multiple_of(n * 384 + i * 48, 16), 48)
+            pieces[8 * n + i, 0:48, :] = part[span, :] + part_rcv[span, :]
+            pieces[8 * n + i, 48:56, :] = both
+        for i in range(8):
+            to = 8 * n + lax.rem(spot + i, 8)
+            send_if(
+                to != spot, PLN + lax.rem(to - spot + 16, 16), pieces.at[to], plane.at[spot],
+                32 * z + 2 * to + core,
+            )
     plane[spot] = pieces[spot]
 
     row_wait(IMG, images, 2, None)
@@ -344,7 +356,8 @@
     for q in (1, 3):
         cross_wait_rest(IMG, images, q, None)
         sib_send(IMG, images, 3 + q, crossed(x, q))
-    image_pair(2)
+    image_pairs(2)
+    image_pairs(4, 6)
 
     for o in range(1, 16):
         arrived(PLN + o, plane.at[lax.rem(spot + 16 - o, 16)])
@@ -365,11 +378,9 @@
         def _():
             owned[z] = tails[j]
 
-    image_pair(4)
-    image_pair(6)
     cross_wait(IMG, images, 2, None)
     sib_send(IMG, images, 5, crossed(x, 2))
-    image_pair(5)
+    image_pairs(5)
     unit = unit_t[...]
     dunit = acc_t[...]
     tg_ref[...] = dunit - unit * jnp.sum(unit * dunit, axis=-1, keepdims=True)

time: 76.4 us -> 74.4 us (0.974)
  Pallas kernels: 74.3 us -> 72.3 us
    pallas_call x1, Pallas kernels: 72.3 us -> 70.3 us  [shards(): pl.pallas_call(kernel, out_shape=(jax.ShapeDtypeStruct((8, 2 * B), f32),...]
where the time goes in v2:
time: 74.4 us; the launch traced here: 74.2 us
  Pallas kernels  72.3 us (97%)
  between operations  1.93 us (3%)
    pallas_call x1, Pallas kernels, shards(): pl.pallas_call(kernel, out_shape=(jax.ShapeDtypeStruct((8, 2 * B), f32),...  70.3 us
    pallas_call x1, Pallas kernels, shards(): pl.pallas_call(finish, out_shape=(jax.ShapeDtypeStruct((1,), f32), jax.Sh...  2.02 us

profile of v2, /device:TPU:1, one launch (start us, length us, event | category | flops | bytes accessed | tf_op | source)
XLA Modules:
  0.0 74.2 jit_solution(7220840347612650923)
XLA Ops:
  1.9 70.3 %contrastive.1 = (f32[8,256]{1,0:T(8,128)}, f32[6,1024]{1,0:T(8,128)}, f32[128,1024]{1,0:T(8,128)}, f32[128,128]{1,0:T(8,128)}) custom-call(f32[1]{0:T(128)S(6)} %copy.10.ls_ref, f32[1]{0:T(128)S(6)} %copy.11.lb_ref, bf16[128,1536]{1,0:T(8,128)(2,1)} %imgf_ref.1, bf16[128,4096]{1,0:T(8,128)(2,1)} %txtf_ref.1, bf16[1536,1024]{1,0:T(8,128)(2,1)} %imgh_ref.1, ...), custom_call_target="tpu_custom_call" | custom-call | flops 5000000000 | bytes 14000000 | tf_op jit(solution)/shard_map/contrastive/pallas_call | solution.py:422
  72.2 2.0 %finish.1 = (f32[1]{0:T(128)}, f32[2]{0:T(128)}, f32[6,1024]{1,0:T(8,128)}, f32[128,1024]{1,0:T(8,128)}) custom-call(f32[1]{0:T(128)S(6)} %copy.10.ls_ref, f32[8,256]{1,0:T(8,128)} %get-tuple-element.12.st_ref, f32[6,1024]{1,0:T(8,128)} %get-tuple-element.13.hgs_ref, f32[128,1024]{1,0:T(8,128)} %get-tuple-element.14.tgs_ref, ...), custom_call_target="tpu_custom_call" | custom-call | tf_op jit(solution)/shard_map/finish/pallas_call | solution.py:466

commit v3 on v2

--- a/solution.py
+++ b/solution.py
@@ -118,6 +118,14 @@
             c.start()
 
         sent_if.append((cond, c))
+
+    def drain(always, perhaps):
+        for c in always:
+            c.wait_send()
+        for cond, c in perhaps:
+            @pl.when(cond)
+            def _():
+                c.wait_send()
 
     def arrived(i, dst):
         copy(i, dst, dst, sib).wait_recv()
@@ -275,13 +283,22 @@
     sib_send(TXT, texts, 2, in_row(x, 2))
     arrived(FEA + 1, fea(1))
     send(FEA + 2, fea(1), fea(2), z_mate(-side))
+    for half in (0, 1):
+        row_send(IMG, images, half)
     text_pairs(1, 3)
-    row_send(IMG, images, None)
     text_pairs(2)
     for q in (1, 3):
         for half in (0, 1):
             cross_wait_rest(TXT, texts, q, half)
         sib_send(TXT, texts, 3 + q, crossed(x, q))
+
+    def image_forward(half):
+        for q in (1, 3):
+            row_wait(IMG, images, q, half)
+            cross_send(IMG, images, q, half)
+        opposite_send(IMG, images, half)
+
+    image_forward(0)
     text_pairs(4, 6)
     for half in (0, 1):
         cross_wait(TXT, texts, 2, half)
@@ -305,14 +322,15 @@
     for n, off in ((1, -side), (2, -2 * side), (3, side)):
         send(DLO + n, dlow_t.at[quarter(off)], window(n), z_mate(off))
     dgat[:, 0:B] = dlow_t[quarter(0)]
-    for q in (1, 3):
-        row_wait(IMG, images, q, None)
-        cross_send(IMG, images, q, None)
-    opposite_send(IMG, images, None)
+    image_forward(1)
     for q in (1, 3):
         sib_send(IMG, images, q, in_row(x, q))
     image_pairs(0)
     image_pairs(1, 3)
+    for half in (0, 1):
+        row_wait(IMG, images, 2, half)
+        cross_send(IMG, images, 2, half)
+    sib_send(IMG, images, 2, in_row(x, 2))
 
     for n in (1, 2, 3):
         arrived(DLO + n, window(n))
@@ -333,6 +351,9 @@
         send(SIB + j, part_rows(part_sib, n), part_rows(part_rcv, n), sib)
     for n in (core, 1 - core):
         product(core, n, part)
+    early, early_if = list(sent), list(sent_if)
+    sent.clear()
+    sent_if.clear()
     arrived(SIB + 2, stats2)
     both = stat[...] + stats2[...]
     for j, n in enumerate((core, 1 - core)):
@@ -349,15 +370,10 @@
             )
     plane[spot] = pieces[spot]
 
-    row_wait(IMG, images, 2, None)
-    cross_send(IMG, images, 2, None)
-    sib_send(IMG, images, 2, in_row(x, 2))
-    hand_on(IMG, images, None)
-    for q in (1, 3):
-        cross_wait_rest(IMG, images, q, None)
-        sib_send(IMG, images, 3 + q, crossed(x, q))
+    for half in (0, 1):
+        hand_on(IMG, images, half)
     image_pairs(2)
-    image_pairs(4, 6)
+    drain(early, early_if)
 
     for o in range(1, 16):
         arrived(PLN + o, plane.at[lax.rem(spot + 16 - o, 16)])
@@ -378,7 +394,13 @@
         def _():
             owned[z] = tails[j]
 
-    cross_wait(IMG, images, 2, None)
+    for q in (1, 3):
+        for half in (0, 1):
+            cross_wait_rest(IMG, images, q, half)
+        sib_send(IMG, images, 3 + q, crossed(x, q))
+    image_pairs(4, 6)
+    for half in (0, 1):
+        cross_wait(IMG, images, 2, half)
     sib_send(IMG, images, 5, crossed(x, 2))
     image_pairs(5)
     unit = unit_t[...]
@@ -397,12 +419,7 @@
         @pl.when(first_owner + j != me)
         def _():
             copy(OWN + j, tails.at[j], owned.at[z], first_owner + j).wait_send()
-    for c in sent:
-        c.wait_send()
-    for cond, c in sent_if:
-        @pl.when(cond)
-        def _():
-            c.wait_send()
+    drain(sent, sent_if)
 
 
 def finish(ls_ref, st_ref, hgs_ref, tgs_ref, tinv_ref, loss_ref, sg_ref, hg_ref, tg_ref):

time: 74.4 us -> 75.4 us (1.013); the launches traced: 74.2 us -> 73.9 us
  no operation moved by 1% of the time
where the time goes in v3:
time: 75.4 us; the launch traced here: 73.9 us
  Pallas kernels  71.9 us (95%)
  between operations  1.93 us (3%)
    pallas_call x1, Pallas kernels, shards(): pl.pallas_call(kernel, out_shape=(jax.ShapeDtypeStruct((8, 2 * B), f32),...  69.9 us
    pallas_call x1, Pallas kernels, shards(): pl.pallas_call(finish, out_shape=(jax.ShapeDtypeStruct((1,), f32), jax.Sh...  2.02 us

profile of v3, /device:TPU:1, one launch (start us, length us, event | category | flops | bytes accessed | tf_op | source)
XLA Modules:
  0.0 73.9 jit_solution(8161931090413791548)
XLA Ops:
  1.9 69.9 %contrastive.1 = (f32[8,256]{1,0:T(8,128)}, f32[6,1024]{1,0:T(8,128)}, f32[128,1024]{1,0:T(8,128)}, f32[128,128]{1,0:T(8,128)}) custom-call(f32[1]{0:T(128)S(6)} %copy.10.ls_ref, f32[1]{0:T(128)S(6)} %copy.11.lb_ref, bf16[128,1536]{1,0:T(8,128)(2,1)} %imgf_ref.1, bf16[128,4096]{1,0:T(8,128)(2,1)} %txtf_ref.1, bf16[1536,1024]{1,0:T(8,128)(2,1)} %imgh_ref.1, ...), custom_call_target="tpu_custom_call" | custom-call | flops 5000000000 | bytes 14000000 | tf_op jit(solution)/shard_map/contrastive/pallas_call | solution.py:439
  71.8 2.0 %finish.1 = (f32[1]{0:T(128)}, f32[2]{0:T(128)}, f32[6,1024]{1,0:T(8,128)}, f32[128,1024]{1,0:T(8,128)}) custom-call(f32[1]{0:T(128)S(6)} %copy.10.ls_ref, f32[8,256]{1,0:T(8,128)} %get-tuple-element.12.st_ref, f32[6,1024]{1,0:T(8,128)} %get-tuple-element.13.hgs_ref, f32[128,1024]{1,0:T(8,128)} %get-tuple-element.14.tgs_ref, ...), custom_call_target="tpu_custom_call" | custom-call | tf_op jit(solution)/shard_map/finish/pallas_call | solution.py:483

commit v4 on v3

--- a/solution.py
+++ b/solution.py
@@ -28,7 +28,7 @@
     ls_ref, lb_ref, imgf_ref, txtf_ref, imgh_ref, txth_ref,
     st_ref, hg_ref, tg_ref, tinv_ref,
     txtf, imgh, txth, feats, texts, images, unit_t, unit_i, acc_t, acc_i, inv_t, inv_i,
-    dlow_t, dgat, stat, stats2, tails, part_sib, part_rcv, part, plane, owned, pieces,
+    sum_t, sum_i, rcv_t, rcv_i, dlow_t, dgat, stat, stats2, tails, part_sib, part_rcv, part, plane, owned, pieces,
     load_sem, send_sem, recv_sem,
 ):
     me = lax.axis_index("dp")
@@ -151,11 +151,15 @@
     def row_wait(base, ref, q, half):
         arrived(base + 2 * (q - 1) + (half or 0), slot(ref, in_row(x, q), half))
 
+    right_on = (x == 3) | ((core == 0) & (x < 2))
+    left_on = (x == 0) | ((core == 1) & (x >= 2))
+
     def opposite_send(base, ref, half):
-        at = lax.rem(x + side + 4, 4)
-        send(
-            base + 2 + (half or 0), slot(ref, in_row(x, 2 + side), half), slot(ref, in_row(at, 2), half),
-            row_first + 2 * at,
+        i = base + 2 + (half or 0)
+        send_if(right_on, i, slot(ref, in_row(x, 3), half), slot(ref, in_row(right_x, 2), half), right)
+        send_if(
+            left_on, base + 21 + (half or 0), slot(ref, in_row(x, 1), half), slot(ref, in_row(left_x, 2), half),
+            left, i,
         )
 
     def cross_send(base, ref, q, half):
@@ -188,11 +192,21 @@
             row_first + 2 * to, base + 8 + (half or 0),
         )
 
-    def sib_send(base, ref, n, off):
-        send(base + 14 + n, slot(ref, off), slot(ref, off), sib)
-
-    def sib_wait(base, ref, n, off):
-        arrived(base + 14 + n, ref.at[2 * (3 + off) + 1 - core])
+    def own_rows(ref, of):
+        return ref.at[pl.ds(pl.multiple_of(of * B, B), B)]
+
+    def own_send(base, ref):
+        send(base + 14, slot(ref, 0), slot(ref, 0), sib)
+
+    def own_wait(base, ref):
+        arrived(base + 14, ref.at[7 - core])
+
+    def sums_send(base, acc, rcv):
+        send(base + 15, own_rows(acc, 1 - core), rcv, sib)
+
+    def sums(base, acc, rcv):
+        arrived(base + 15, rcv)
+        return own_rows(acc, core)[...] + rcv[...]
 
     def project(read, head, acc, first, count):
         acc[...] = jnp.zeros((B, E), jnp.float32)
@@ -209,109 +223,97 @@
         ref[6 + core] = value.astype(jnp.bfloat16)
 
     loads[1].wait()
-    project(lambda j: txtf[:, pl.ds(j * CH, CH)], txth, acc_t, 2, DT // CH)
-    normalize(acc_t, unit_t, inv_t, texts)
+    project(lambda j: txtf[:, pl.ds(j * CH, CH)], txth, sum_t, 2, DT // CH)
+    normalize(sum_t, unit_t, inv_t, texts)
     pl.semaphore_wait(barrier, 23 + 8 - owner_is_me.astype(jnp.int32))
     for half in (0, 1):
         row_send(TXT, texts, half)
-    sib_send(TXT, texts, 0, 0)
+    own_send(TXT, texts)
     loads[0].wait()
     send(FEA + 1, fea(0), fea(1), z_mate(-side))
     send(FEA + 3, fea(0), fea(3), z_mate(side))
-    project(lambda j: feats[pl.ds(0, B), pl.ds(j * CH, CH)], imgh, acc_i, 10, DI // CH)
-    normalize(acc_i, unit_i, inv_i, images)
-    sib_send(IMG, images, 0, 0)
+    project(lambda j: feats[pl.ds(0, B), pl.ds(j * CH, CH)], imgh, sum_i, 10, DI // CH)
+    normalize(sum_i, unit_i, inv_i, images)
+    own_send(IMG, images)
 
     temper = jnp.exp(jnp.full((1, 2 * B), ls_ref[0], jnp.float32))
     bias = lb_ref[0]
-    rows = lax.broadcasted_iota(jnp.int32, (B, 2 * B), 0)
-    cols = lax.broadcasted_iota(jnp.int32, (B, 2 * B), 1)
-    acc_i[...] = jnp.zeros((B, E), jnp.float32)
-    acc_t[...] = jnp.zeros((B, E), jnp.float32)
-    totals = [jnp.zeros((1, 2 * B), jnp.float32) for _ in range(3)]
-
-    def pairs(base, own, ref, numbers, acc, stats):
+    rows = lax.broadcasted_iota(jnp.int32, (2 * B, 1), 0)
+    acc_i[...] = jnp.zeros((2 * B, E), jnp.float32)
+    acc_t[...] = jnp.zeros((2 * B, E), jnp.float32)
+    totals = [jnp.zeros((1, B), jnp.float32) for _ in range(3)]
+    far_row = jnp.where((rows >= B) == (core == 0), 1.0, 0.0)
+
+    def group(own, ref, numbers, acc, stats):
         offs = [0 if n == 0 else in_row(x, n) if n < 4 else crossed(x, n - 3) for n in numbers]
-        for n, off in zip(numbers, offs):
-            sib_wait(base, ref, n, off)
-        added = None
-        for n, off in zip(numbers, offs):
-            block = ref[pl.ds(2 * (3 + off), 2)].reshape(2 * B, E)
-            cosine = lax.dot_general(
-                own[6 + core], block, (((1,), (1,)), ((), ())), preferred_element_type=jnp.float32
+        wide = B * len(offs)
+        block = jnp.concatenate([slot(ref, off)[...] for off in offs], axis=0)
+        both = own[6:8].reshape(2 * B, E)
+        cosine = lax.dot_general(
+            both, block, (((1,), (1,)), ((), ())), preferred_element_type=jnp.float32
+        )
+        logits = temper[:, :wide] * cosine + bias
+        small = jnp.exp(-jnp.abs(logits))
+        grad = jnp.where(logits >= 0.0, 1.0, small) / (1.0 + small)
+        if numbers == (0,):
+            hit = lax.broadcasted_iota(jnp.int32, (2 * B, B), 1) + core * B == rows
+            grad = grad - jnp.where(hit, 1.0, 0.0)
+        else:
+            far = jnp.concatenate(
+                [jnp.full((1, B), (off == 6 * core - 3).astype(jnp.float32)) for off in offs], axis=1
             )
-            logits = temper * cosine + bias
-            small = jnp.exp(-jnp.abs(logits))
-            grad = jnp.where(logits >= 0.0, 1.0, small) / (1.0 + small)
-            if n == 0:
-                hit = cols == rows + core * B
-                grad = grad - jnp.where(hit, 1.0, 0.0)
-            else:
-                apart = 2 * off - core + (cols >= B).astype(jnp.int32)
-                valid = (apart >= -6) & (apart <= 6)
-                grad = jnp.where(valid, grad, 0.0)
-            if stats:
-                signed = jnp.where(hit, -logits, logits) if n == 0 else logits
-                loss = jnp.maximum(signed, 0.0) + jnp.log1p(small)
-                if n > 0:
-                    loss = jnp.where(valid, loss, 0.0)
-                for k, term in enumerate((loss, grad * cosine, grad)):
-                    totals[k] = totals[k] + jnp.sum(term, axis=0, keepdims=True)
-            weights = (temper * grad).astype(jnp.bfloat16)
-            term = jnp.dot(weights, block, preferred_element_type=jnp.float32)
-            added = term if added is None else added + term
-        acc[...] += added
-
-    def text_pairs(*numbers):
-        pairs(TXT, images, texts, numbers, acc_i, True)
-
-    def image_pairs(*numbers):
-        pairs(IMG, texts, images, numbers, acc_t, False)
-
-    text_pairs(0)
+            live = 1.0 - far_row * far
+            grad = grad * live
+        if stats:
+            signed = jnp.where(hit, -logits, logits) if numbers == (0,) else logits
+            loss = jnp.maximum(signed, 0.0) + jnp.log1p(small)
+            if numbers != (0,):
+                loss = loss * live
+            for k, term in enumerate((loss, grad * cosine, grad)):
+                term = jnp.sum(term, axis=0, keepdims=True)
+                for n in range(len(offs)):
+                    totals[k] = totals[k] + term[:, n * B : (n + 1) * B]
+        weights = (temper[:, :wide] * grad).astype(jnp.bfloat16)
+        acc[...] += jnp.dot(weights, block, preferred_element_type=jnp.float32)
+
+    def text_group(*numbers):
+        group(images, texts, numbers, acc_i, True)
+
+    def image_group(*numbers):
+        group(texts, images, numbers, acc_t, False)
+
+    own_wait(IMG, images)
+    text_group(0)
     for half in (0, 1):
         for q in (1, 3):
             row_wait(TXT, texts, q, half)
             cross_send(TXT, texts, q, half)
         opposite_send(TXT, texts, half)
-    for q in (1, 3):
-        sib_send(TXT, texts, q, in_row(x, q))
     for half in (0, 1):
         row_wait(TXT, texts, 2, half)
         cross_send(TXT, texts, 2, half)
         hand_on(TXT, texts, half)
-    sib_send(TXT, texts, 2, in_row(x, 2))
+    row_send(IMG, images, None)
     arrived(FEA + 1, fea(1))
     send(FEA + 2, fea(1), fea(2), z_mate(-side))
-    for half in (0, 1):
-        row_send(IMG, images, half)
-    text_pairs(1, 3)
-    text_pairs(2)
+    text_group(1, 3)
+    text_group(2)
     for q in (1, 3):
         for half in (0, 1):
             cross_wait_rest(TXT, texts, q, half)
-        sib_send(TXT, texts, 3 + q, crossed(x, q))
-
-    def image_forward(half):
-        for q in (1, 3):
-            row_wait(IMG, images, q, half)
-            cross_send(IMG, images, q, half)
-        opposite_send(IMG, images, half)
-
-    image_forward(0)
-    text_pairs(4, 6)
+    text_group(4, 6)
     for half in (0, 1):
         cross_wait(TXT, texts, 2, half)
-    sib_send(TXT, texts, 5, crossed(x, 2))
-    text_pairs(5)
+    text_group(5)
+    sums_send(TXT, acc_i, rcv_i)
 
     stat[...] = jnp.zeros((8, 2 * B), jnp.float32)
-    stat[0:1, 0:B] = totals[0][:, :B] + totals[0][:, B:]
-    stat[0:1, B : 2 * B] = totals[1][:, :B] + totals[1][:, B:]
-    stat[1:2, 0:B] = totals[2][:, :B] + totals[2][:, B:]
+    stat[0:1, 0:B] = totals[0]
+    stat[0:1, B : 2 * B] = totals[1]
+    stat[1:2, 0:B] = totals[2]
     send(SIB + 2, stat, stats2, sib)
     unit = unit_i[...]
-    dunit = acc_i[...]
+    dunit = sums(TXT, acc_i, rcv_i)
     dproj = inv_i[:, 0:1] * (dunit - unit * jnp.sum(unit * dunit, axis=-1, keepdims=True))
     for j in range(4):
         dlow_t[j] = dproj[:, j * 256 : (j + 1) * 256].T.astype(jnp.bfloat16)
@@ -322,15 +324,15 @@
     for n, off in ((1, -side), (2, -2 * side), (3, side)):
         send(DLO + n, dlow_t.at[quarter(off)], window(n), z_mate(off))
     dgat[:, 0:B] = dlow_t[quarter(0)]
-    image_forward(1)
     for q in (1, 3):
-        sib_send(IMG, images, q, in_row(x, q))
-    image_pairs(0)
-    image_pairs(1, 3)
-    for half in (0, 1):
-        row_wait(IMG, images, 2, half)
-        cross_send(IMG, images, 2, half)
-    sib_send(IMG, images, 2, in_row(x, 2))
+        row_wait(IMG, images, q, None)
+        cross_send(IMG, images, q, None)
+    opposite_send(IMG, images, None)
+    own_wait(TXT, texts)
+    image_group(0)
+    image_group(1, 3)
+    row_wait(IMG, images, 2, None)
+    cross_send(IMG, images, 2, None)
 
     for n in (1, 2, 3):
         arrived(DLO + n, window(n))
@@ -370,9 +372,8 @@
             )
     plane[spot] = pieces[spot]
 
-    for half in (0, 1):
-        hand_on(IMG, images, half)
-    image_pairs(2)
+    hand_on(IMG, images, None)
+    image_group(2)
     drain(early, early_if)
 
     for o in range(1, 16):
@@ -395,16 +396,13 @@
             owned[z] = tails[j]
 
     for q in (1, 3):
-        for half in (0, 1):
-            cross_wait_rest(IMG, images, q, half)
-        sib_send(IMG, images, 3 + q, crossed(x, q))
-    image_pairs(4, 6)
-    for half in (0, 1):
-        cross_wait(IMG, images, 2, half)
-    sib_send(IMG, images, 5, crossed(x, 2))
-    image_pairs(5)
+        cross_wait_rest(IMG, images, q, None)
+    image_group(4, 6)
+    cross_wait(IMG, images, 2, None)
+    image_group(5)
+    sums_send(IMG, acc_t, rcv_t)
     unit = unit_t[...]
-    dunit = acc_t[...]
+    dunit = sums(IMG, acc_t, rcv_t)
     tg_ref[...] = dunit - unit * jnp.sum(unit * dunit, axis=-1, keepdims=True)
     tinv_ref[...] = inv_t[...]
 
@@ -455,10 +453,14 @@
             pltpu.VMEM((14, B, E), bf16),
             pltpu.VMEM((B, E), f32),
             pltpu.VMEM((B, E), f32),
+            pltpu.VMEM((2 * B, E), f32),
+            pltpu.VMEM((2 * B, E), f32),
+            pltpu.VMEM((B, 128), f32),
+            pltpu.VMEM((B, 128), f32),
             pltpu.VMEM((B, E), f32),
             pltpu.VMEM((B, E), f32),
-            pltpu.VMEM((B, 128), f32),
-            pltpu.VMEM((B, 128), f32),
+            pltpu.VMEM((B, E), f32),
+            pltpu.VMEM((B, E), f32),
             pltpu.VMEM((4, 256, B), bf16),
             pltpu.VMEM((256, 4 * B), bf16),
             pltpu.VMEM((8, 256), f32),

time: 75.4 us -> 74.6 us (0.989); the launches traced: 73.9 us -> 74.4 us
  no operation moved by 1% of the time
where the time goes in v4:
time: 74.6 us; the launch traced here: 74.4 us
  Pallas kernels  72.4 us (97%)
  between operations  1.93 us (3%)
    pallas_call x1, Pallas kernels, shards(): pl.pallas_call(kernel, out_shape=(jax.ShapeDtypeStruct((8, 2 * B), f32),...  70.4 us
    pallas_call x1, Pallas kernels, shards(): pl.pallas_call(finish, out_shape=(jax.ShapeDtypeStruct((1,), f32), jax.Sh...  2.02 us

profile of v4, /device:TPU:1, one launch (start us, length us, event | category | flops | bytes accessed | tf_op | source)
XLA Modules:
  0.0 74.4 jit_solution(1273967161251577537)
XLA Ops:
  1.9 70.4 %contrastive.1 = (f32[8,256]{1,0:T(8,128)}, f32[6,1024]{1,0:T(8,128)}, f32[128,1024]{1,0:T(8,128)}, f32[128,128]{1,0:T(8,128)}) custom-call(f32[1]{0:T(128)S(6)} %copy.10.ls_ref, f32[1]{0:T(128)S(6)} %copy.11.lb_ref, bf16[128,1536]{1,0:T(8,128)(2,1)} %imgf_ref.1, bf16[128,4096]{1,0:T(8,128)(2,1)} %txtf_ref.1, bf16[1536,1024]{1,0:T(8,128)(2,1)} %imgh_ref.1, ...), custom_call_target="tpu_custom_call" | custom-call | flops 5000000000 | bytes 14000000 | tf_op jit(solution)/shard_map/contrastive/pallas_call | solution.py:437
  72.3 2.0 %finish.1 = (f32[1]{0:T(128)}, f32[2]{0:T(128)}, f32[6,1024]{1,0:T(8,128)}, f32[128,1024]{1,0:T(8,128)}) custom-call(f32[1]{0:T(128)S(6)} %copy.10.ls_ref, f32[8,256]{1,0:T(8,128)} %get-tuple-element.12.st_ref, f32[6,1024]{1,0:T(8,128)} %get-tuple-element.13.hgs_ref, f32[128,1024]{1,0:T(8,128)} %get-tuple-element.14.tgs_ref, ...), custom_call_target="tpu_custom_call" | custom-call | tf_op jit(solution)/shard_map/finish/pallas_call | solution.py:485

commit v5 on v4

--- a/solution.py
+++ b/solution.py
@@ -293,7 +293,8 @@
         row_wait(TXT, texts, 2, half)
         cross_send(TXT, texts, 2, half)
         hand_on(TXT, texts, half)
-    row_send(IMG, images, None)
+    for half in (0, 1):
+        row_send(IMG, images, half)
     arrived(FEA + 1, fea(1))
     send(FEA + 2, fea(1), fea(2), z_mate(-side))
     text_group(1, 3)
@@ -301,11 +302,23 @@
     for q in (1, 3):
         for half in (0, 1):
             cross_wait_rest(TXT, texts, q, half)
+    early, early_if = list(sent), list(sent_if)
+    sent.clear()
+    sent_if.clear()
+
+    def image_forward(half):
+        for q in (1, 3):
+            row_wait(IMG, images, q, half)
+            cross_send(IMG, images, q, half)
+        opposite_send(IMG, images, half)
+
+    image_forward(0)
     text_group(4, 6)
     for half in (0, 1):
         cross_wait(TXT, texts, 2, half)
     text_group(5)
     sums_send(TXT, acc_i, rcv_i)
+    image_forward(1)
 
     stat[...] = jnp.zeros((8, 2 * B), jnp.float32)
     stat[0:1, 0:B] = totals[0]
@@ -324,15 +337,12 @@
     for n, off in ((1, -side), (2, -2 * side), (3, side)):
         send(DLO + n, dlow_t.at[quarter(off)], window(n), z_mate(off))
     dgat[:, 0:B] = dlow_t[quarter(0)]
-    for q in (1, 3):
-        row_wait(IMG, images, q, None)
-        cross_send(IMG, images, q, None)
-    opposite_send(IMG, images, None)
     own_wait(TXT, texts)
     image_group(0)
     image_group(1, 3)
-    row_wait(IMG, images, 2, None)
-    cross_send(IMG, images, 2, None)
+    for half in (0, 1):
+        row_wait(IMG, images, 2, half)
+        cross_send(IMG, images, 2, half)
 
     for n in (1, 2, 3):
         arrived(DLO + n, window(n))
@@ -353,9 +363,6 @@
         send(SIB + j, part_rows(part_sib, n), part_rows(part_rcv, n), sib)
     for n in (core, 1 - core):
         product(core, n, part)
-    early, early_if = list(sent), list(sent_if)
-    sent.clear()
-    sent_if.clear()
     arrived(SIB + 2, stats2)
     both = stat[...] + stats2[...]
     for j, n in enumerate((core, 1 - core)):
@@ -372,7 +379,8 @@
             )
     plane[spot] = pieces[spot]
 
-    hand_on(IMG, images, None)
+    for half in (0, 1):
+        hand_on(IMG, images, half)
     image_group(2)
     drain(early, early_if)
 
@@ -396,9 +404,11 @@
             owned[z] = tails[j]
 
     for q in (1, 3):
-        cross_wait_rest(IMG, images, q, None)
+        for half in (0, 1):
+            cross_wait_rest(IMG, images, q, half)
     image_group(4, 6)
-    cross_wait(IMG, images, 2, None)
+    for half in (0, 1):
+        cross_wait(IMG, images, 2, half)
     image_group(5)
     sums_send(IMG, acc_t, rcv_t)
     unit = unit_t[...]

time: 74.6 us -> 81.1 us (1.087)
  the two profiles are of different devices: /device:TPU:1 before, /device:TPU:81 now
where the time goes in v5:
time: 81.1 us; the launch traced here: 80.9 us
  Pallas kernels  79 us (97%)
  between operations  1.93 us (2%)
    pallas_call x1, Pallas kernels, shards(): pl.pallas_call(kernel, out_shape=(jax.ShapeDtypeStruct((8, 2 * B), f32),...  77 us
    pallas_call x1, Pallas kernels, shards(): pl.pallas_call(finish, out_shape=(jax.ShapeDtypeStruct((1,), f32), jax.Sh...  2.02 us

profile of v5, /device:TPU:81, one launch (start us, length us, event | category | flops | bytes accessed | tf_op | source)
XLA Modules:
  0.0 80.9 jit_solution(9097782251302716705)
XLA Ops:
  1.9 77.0 %contrastive.1 = (f32[8,256]{1,0:T(8,128)}, f32[6,1024]{1,0:T(8,128)}, f32[128,1024]{1,0:T(8,128)}, f32[128,128]{1,0:T(8,128)}) custom-call(f32[1]{0:T(128)S(6)} %copy.10.ls_ref, f32[1]{0:T(128)S(6)} %copy.11.lb_ref, bf16[128,1536]{1,0:T(8,128)(2,1)} %imgf_ref.1, bf16[128,4096]{1,0:T(8,128)(2,1)} %txtf_ref.1, bf16[1536,1024]{1,0:T(8,128)(2,1)} %imgh_ref.1, ...), custom_call_target="tpu_custom_call" | custom-call | flops 5000000000 | bytes 14000000 | tf_op jit(solution)/shard_map/contrastive/pallas_call | solution.py:447
  78.9 2.0 %finish.1 = (f32[1]{0:T(128)}, f32[2]{0:T(128)}, f32[6,1024]{1,0:T(8,128)}, f32[128,1024]{1,0:T(8,128)}) custom-call(f32[1]{0:T(128)S(6)} %copy.10.ls_ref, f32[8,256]{1,0:T(8,128)} %get-tuple-element.12.st_ref, f32[6,1024]{1,0:T(8,128)} %get-tuple-element.13.hgs_ref, f32[128,1024]{1,0:T(8,128)} %get-tuple-element.14.tgs_ref, ...), custom_call_target="tpu_custom_call" | custom-call | tf_op jit(solution)/shard_map/finish/pallas_call | solution.py:495

commit v6 on v4

--- a/solution.py
+++ b/solution.py
@@ -19,7 +19,8 @@
 FEA = 48
 DLO = 52
 SIB = 56
-PLN = 60
+PLA = 60
+PLB = 68
 OWN = 76
 IDS = 84
 
@@ -28,7 +29,8 @@
     ls_ref, lb_ref, imgf_ref, txtf_ref, imgh_ref, txth_ref,
     st_ref, hg_ref, tg_ref, tinv_ref,
     txtf, imgh, txth, feats, texts, images, unit_t, unit_i, acc_t, acc_i, inv_t, inv_i,
-    sum_t, sum_i, rcv_t, rcv_i, dlow_t, dgat, stat, stats2, tails, part_sib, part_rcv, part, plane, owned, pieces,
+    sum_t, sum_i, rcv_t, rcv_i, dlow_t, dgat, stat, stats2, tails, part_sib, part_rcv, part, owned,
+    out_a, in_a, out_b, in_b, out_a2, in_a2, out_b2, in_b2,
     load_sem, send_sem, recv_sem,
 ):
     me = lax.axis_index("dp")
@@ -54,8 +56,13 @@
     def quarter(off):
         return lax.rem(z + off + 8, 4)
 
-    def plane_mate(off):
-        return 32 * z + 2 * lax.rem(spot + off, 16) + core
+    y = spot // 4
+
+    def x_mate(off):
+        return row_first + 2 * lax.rem(x + off, 4)
+
+    def y_mate(off):
+        return 32 * z + 8 * lax.rem(y + off, 4) + 2 * x + core
 
     first_owner = 128 * core + 8 * spot
     my_row = me // 8
@@ -70,7 +77,7 @@
     def greet(dev):
         pl.semaphore_signal(barrier, inc=1, device_id={"dp": dev}, device_id_type=pl.DeviceIdType.MESH)
 
-    for dev in [right, left, up, down, sib] + [z_mate(side), z_mate(2 * side), z_mate(-side)] + [plane_mate(o) for o in range(1, 16)]:
+    for dev in [right, left, up, down, sib, x_mate(2)] + [z_mate(side), z_mate(2 * side), z_mate(-side)] + [y_mate(o) for o in range(1, 4)]:
         greet(dev)
     for zz in range(8):
         @pl.when(source(zz) != me)
@@ -225,7 +232,7 @@
     loads[1].wait()
     project(lambda j: txtf[:, pl.ds(j * CH, CH)], txth, sum_t, 2, DT // CH)
     normalize(sum_t, unit_t, inv_t, texts)
-    pl.semaphore_wait(barrier, 23 + 8 - owner_is_me.astype(jnp.int32))
+    pl.semaphore_wait(barrier, 12 + 8 - owner_is_me.astype(jnp.int32))
     for half in (0, 1):
         row_send(TXT, texts, half)
     own_send(TXT, texts)
@@ -307,10 +314,9 @@
     text_group(5)
     sums_send(TXT, acc_i, rcv_i)
 
-    stat[...] = jnp.zeros((8, 2 * B), jnp.float32)
-    stat[0:1, 0:B] = totals[0]
-    stat[0:1, B : 2 * B] = totals[1]
-    stat[1:2, 0:B] = totals[2]
+    for n in range(3):
+        stat[n : n + 1, :] = totals[n]
+    stat[3:8, :] = jnp.zeros((5, B), jnp.float32)
     send(SIB + 2, stat, stats2, sib)
     unit = unit_i[...]
     dunit = sums(TXT, acc_i, rcv_i)
@@ -324,6 +330,9 @@
     for n, off in ((1, -side), (2, -2 * side), (3, side)):
         send(DLO + n, dlow_t.at[quarter(off)], window(n), z_mate(off))
     dgat[:, 0:B] = dlow_t[quarter(0)]
+    early, early_if = list(sent), list(sent_if)
+    sent.clear()
+    sent_if.clear()
     for q in (1, 3):
         row_wait(IMG, images, q, None)
         cross_send(IMG, images, q, None)
@@ -353,35 +362,54 @@
         send(SIB + j, part_rows(part_sib, n), part_rows(part_rcv, n), sib)
     for n in (core, 1 - core):
         product(core, n, part)
-    early, early_if = list(sent), list(sent_if)
-    sent.clear()
-    sent_if.clear()
     arrived(SIB + 2, stats2)
     both = stat[...] + stats2[...]
     for j, n in enumerate((core, 1 - core)):
         arrived(SIB + j, part_rows(part_rcv, n))
         for i in range(8):
             span = pl.ds(pl.multiple_of(n * 384 + i * 48, 16), 48)
-            pieces[8 * n + i, 0:48, :] = part[span, :] + part_rcv[span, :]
-            pieces[8 * n + i, 48:56, :] = both
-        for i in range(8):
-            to = 8 * n + lax.rem(spot + i, 8)
-            send_if(
-                to != spot, PLN + lax.rem(to - spot + 16, 16), pieces.at[to], plane.at[spot],
-                32 * z + 2 * to + core,
-            )
-    plane[spot] = pieces[spot]
+            value = part[span, :] + part_rcv[span, :]
+            to_y, to_x = 2 * n + i // 4, i % 4
+            out_a[to_x, pl.ds(pl.multiple_of(to_y * 48, 16), 48), :] = value[:, :B]
+            out_b[to_y, 48 * to_x : 48 * to_x + 48, :] = value[:, B:]
+        for i in range(2):
+            to_y = 2 * n + i
+            o = lax.rem(to_y - y + 4, 4)
+            send_if(to_y != y, PLB + o, out_b.at[to_y], in_b.at[o], y_mate(o))
+    for n in range(4):
+        out_a[n, 192:200, :] = both
+    for o in (1, 2, 3):
+        send(PLA + o, out_a.at[lax.rem(x + o, 4)], in_a.at[o], x_mate(o))
 
     hand_on(IMG, images, None)
     image_group(2)
     drain(early, early_if)
 
-    for o in range(1, 16):
-        arrived(PLN + o, plane.at[lax.rem(spot + 16 - o, 16)])
-    total = jnp.sum(plane[...], axis=0)
+    def summed(base, out, at, got):
+        for o in (1, 2, 3):
+            arrived(base + o, got.at[o])
+        return out[at] + got[1] + got[2] + got[3]
+
+    total = summed(PLB, out_b, y, in_b)
+    for n in range(4):
+        out_b2[n] = total[48 * n : 48 * n + 48, :]
+    for o in (1, 2, 3):
+        send(PLB + 4 + o, out_b2.at[lax.rem(x + o, 4)], in_b2.at[o], x_mate(o))
+    total = summed(PLA, out_a, x, in_a)
+    for n in range(4):
+        out_a2[n, 0:48, :] = total[48 * n : 48 * n + 48, :]
+        out_a2[n, 48:56, :] = total[192:200, :]
+    for o in (1, 2, 3):
+        send(PLA + 4 + o, out_a2.at[lax.rem(y + o, 4)], in_a2.at[o], y_mate(o))
+    total_b = summed(PLB + 4, out_b2, x, in_b2)
+    total_a = summed(PLA + 4, out_a2, y, in_a2)
     for j in range(8):
-        tails[j, 0:6, :] = total[6 * j : 6 * j + 6, :]
-        tails[j, 6:8, :] = total[48:50, :]
+        tails[j, 0:6, 0:B] = total_a[6 * j : 6 * j + 6, :]
+        tails[j, 0:6, B : 2 * B] = total_b[6 * j : 6 * j + 6, :]
+        tails[j, 6:7, 0:B] = total_a[48:49, :]
+        tails[j, 6:7, B : 2 * B] = total_a[49:50, :]
+        tails[j, 7:8, 0:B] = total_a[50:51, :]
+        tails[j, 7:8, B : 2 * B] = jnp.zeros((1, B), jnp.float32)
     for j in range(8):
         @pl.when(first_owner + j != me)
         def _():
@@ -463,15 +491,21 @@
             pltpu.VMEM((B, E), f32),
             pltpu.VMEM((4, 256, B), bf16),
             pltpu.VMEM((256, 4 * B), bf16),
-            pltpu.VMEM((8, 256), f32),
-            pltpu.VMEM((8, 256), f32),
+            pltpu.VMEM((8, 128), f32),
+            pltpu.VMEM((8, 128), f32),
             pltpu.VMEM((8, 8, 256), f32),
             pltpu.VMEM((768, 256), f32),
             pltpu.VMEM((768, 256), f32),
             pltpu.VMEM((768, 256), f32),
-            pltpu.VMEM((16, 56, 256), f32),
             pltpu.VMEM((8, 8, 256), f32),
-            pltpu.VMEM((16, 56, 256), f32),
+            pltpu.VMEM((4, 200, 128), f32),
+            pltpu.VMEM((4, 200, 128), f32),
+            pltpu.VMEM((4, 192, 128), f32),
+            pltpu.VMEM((4, 192, 128), f32),
+            pltpu.VMEM((4, 56, 128), f32),
+            pltpu.VMEM((4, 56, 128), f32),
+            pltpu.VMEM((4, 48, 128), f32),
+            pltpu.VMEM((4, 48, 128), f32),
             pltpu.SemaphoreType.DMA((16,)),
             pltpu.SemaphoreType.DMA((IDS,)),
             pltpu.SemaphoreType.DMA((IDS,)),

time: 74.6 us -> 72.2 us (0.968)
  Pallas kernels: 72.4 us -> 69.9 us
    pallas_call x1, Pallas kernels: 70.4 us -> 67.8 us  [shards(): pl.pallas_call(kernel, out_shape=(jax.ShapeDtypeStruct((8, 2 * B), f32),...]
where the time goes in v6:
time: 72.2 us; the launch traced here: 71.8 us
  Pallas kernels  69.9 us (97%)
  between operations  1.93 us (3%)
    pallas_call x1, Pallas kernels, shards(): pl.pallas_call(kernel, out_shape=(jax.ShapeDtypeStruct((8, 2 * B), f32),...  67.8 us
    pallas_call x1, Pallas kernels, shards(): pl.pallas_call(finish, out_shape=(jax.ShapeDtypeStruct((1,), f32), jax.Sh...  2.02 us

profile of v6, /device:TPU:1, one launch (start us, length us, event | category | flops | bytes accessed | tf_op | source)
XLA Modules:
  0.0 71.8 jit_solution(18115233477830828086)
XLA Ops:
  1.9 67.8 %contrastive.1 = (f32[8,256]{1,0:T(8,128)}, f32[6,1024]{1,0:T(8,128)}, f32[128,1024]{1,0:T(8,128)}, f32[128,128]{1,0:T(8,128)}) custom-call(f32[1]{0:T(128)S(6)} %copy.10.ls_ref, f32[1]{0:T(128)S(6)} %copy.11.lb_ref, bf16[128,1536]{1,0:T(8,128)(2,1)} %imgf_ref.1, bf16[128,4096]{1,0:T(8,128)(2,1)} %txtf_ref.1, bf16[1536,1024]{1,0:T(8,128)(2,1)} %imgh_ref.1, ...), custom_call_target="tpu_custom_call" | custom-call | flops 5000000000 | bytes 14000000 | tf_op jit(solution)/shard_map/contrastive/pallas_call | solution.py:465
  69.8 2.0 %finish.1 = (f32[1]{0:T(128)}, f32[2]{0:T(128)}, f32[6,1024]{1,0:T(8,128)}, f32[128,1024]{1,0:T(8,128)}) custom-call(f32[1]{0:T(128)S(6)} %copy.10.ls_ref, f32[8,256]{1,0:T(8,128)} %get-tuple-element.12.st_ref, f32[6,1024]{1,0:T(8,128)} %get-tuple-element.13.hgs_ref, f32[128,1024]{1,0:T(8,128)} %get-tuple-element.14.tgs_ref, ...), custom_call_target="tpu_custom_call" | custom-call | tf_op jit(solution)/shard_map/finish/pallas_call | solution.py:519

commit v7 on v6

--- a/solution.py
+++ b/solution.py
@@ -29,7 +29,7 @@
     ls_ref, lb_ref, imgf_ref, txtf_ref, imgh_ref, txth_ref,
     st_ref, hg_ref, tg_ref, tinv_ref,
     txtf, imgh, txth, feats, texts, images, unit_t, unit_i, acc_t, acc_i, inv_t, inv_i,
-    sum_t, sum_i, rcv_t, rcv_i, dlow_t, dgat, stat, stats2, tails, part_sib, part_rcv, part, owned,
+    sum_t, sum_i, rcv_t, rcv_i, dlow, dlow_t, dgat, stat, stats2, tails, part_sib, part_rcv, part, owned,
     out_a, in_a, out_b, in_b, out_a2, in_a2, out_b2, in_b2,
     load_sem, send_sem, recv_sem,
 ):
@@ -72,18 +72,6 @@
     def source(zz):
         return 32 * zz + 2 * src_spot + src_core
 
-    barrier = pltpu.get_barrier_semaphore()
-
-    def greet(dev):
-        pl.semaphore_signal(barrier, inc=1, device_id={"dp": dev}, device_id_type=pl.DeviceIdType.MESH)
-
-    for dev in [right, left, up, down, sib, x_mate(2)] + [z_mate(side), z_mate(2 * side), z_mate(-side)] + [y_mate(o) for o in range(1, 4)]:
-        greet(dev)
-    for zz in range(8):
-        @pl.when(source(zz) != me)
-        def _():
-            greet(source(zz))
-
     loads = {}
 
     def load(i, src, dst):
@@ -96,6 +84,18 @@
         load(2 + j, txth_ref.at[pl.ds(j * CH, CH)], txth.at[pl.ds(j * CH, CH)])
     for j in range(DI // CH):
         load(10 + j, imgh_ref.at[pl.ds(j * CH, CH)], imgh.at[pl.ds(j * CH, CH)])
+
+    barrier = pltpu.get_barrier_semaphore()
+
+    def greet(dev):
+        pl.semaphore_signal(barrier, inc=1, device_id={"dp": dev}, device_id_type=pl.DeviceIdType.MESH)
+
+    for dev in [right, left, up, down, sib, x_mate(2)] + [z_mate(side), z_mate(2 * side), z_mate(-side)] + [y_mate(o) for o in range(1, 4)]:
+        greet(dev)
+    for zz in range(8):
+        @pl.when(source(zz) != me)
+        def _():
+            greet(source(zz))
 
     owner_is_me = (me >= first_owner) & (me < first_owner + 8)
 
@@ -321,15 +321,19 @@
     unit = unit_i[...]
     dunit = sums(TXT, acc_i, rcv_i)
     dproj = inv_i[:, 0:1] * (dunit - unit * jnp.sum(unit * dunit, axis=-1, keepdims=True))
-    for j in range(4):
-        dlow_t[j] = dproj[:, j * 256 : (j + 1) * 256].T.astype(jnp.bfloat16)
+    dlow[...] = dproj
 
     def window(n):
         return dgat.at[:, pl.ds(n * B, B)]
 
-    for n, off in ((1, -side), (2, -2 * side), (3, side)):
-        send(DLO + n, dlow_t.at[quarter(off)], window(n), z_mate(off))
-    dgat[:, 0:B] = dlow_t[quarter(0)]
+    for n, off in ((2, -2 * side), (1, -side), (3, side), (0, 0)):
+        j = quarter(off)
+        turned = dlow[:, pl.ds(pl.multiple_of(j * 256, 256), 256)].T.astype(jnp.bfloat16)
+        if n == 0:
+            dgat[:, 0:B] = turned
+        else:
+            dlow_t[n] = turned
+            send(DLO + n, dlow_t.at[n], window(n), z_mate(off))
     early, early_if = list(sent), list(sent_if)
     sent.clear()
     sent_if.clear()
@@ -340,8 +344,6 @@
     own_wait(TXT, texts)
     image_group(0)
     image_group(1, 3)
-    row_wait(IMG, images, 2, None)
-    cross_send(IMG, images, 2, None)
 
     for n in (1, 2, 3):
         arrived(DLO + n, window(n))
@@ -381,6 +383,8 @@
     for o in (1, 2, 3):
         send(PLA + o, out_a.at[lax.rem(x + o, 4)], in_a.at[o], x_mate(o))
 
+    row_wait(IMG, images, 2, None)
+    cross_send(IMG, images, 2, None)
     hand_on(IMG, images, None)
     image_group(2)
     drain(early, early_if)
@@ -485,6 +489,7 @@
             pltpu.VMEM((2 * B, E), f32),
             pltpu.VMEM((B, 128), f32),
             pltpu.VMEM((B, 128), f32),
+            pltpu.VMEM((B, E), f32),
             pltpu.VMEM((B, E), f32),
             pltpu.VMEM((B, E), f32),
             pltpu.VMEM((B, E), f32),

time: 72.2 us -> 72.1 us (level)
  no operation moved by 1% of the time
where the time goes in v7:
time: 72.1 us; the launch traced here: 71.8 us
  Pallas kernels  69.9 us (97%)
  between operations  1.93 us (3%)
    pallas_call x1, Pallas kernels, shards(): pl.pallas_call(kernel, out_shape=(jax.ShapeDtypeStruct((8, 2 * B), f32),...  67.8 us
    pallas_call x1, Pallas kernels, shards(): pl.pallas_call(finish, out_shape=(jax.ShapeDtypeStruct((1,), f32), jax.Sh...  2.02 us

profile of v7, /device:TPU:1, one launch (start us, length us, event | category | flops | bytes accessed | tf_op | source)
XLA Modules:
  0.0 71.8 jit_solution(1222519182382245831)
XLA Ops:
  1.9 67.8 %contrastive.1 = (f32[8,256]{1,0:T(8,128)}, f32[6,1024]{1,0:T(8,128)}, f32[128,1024]{1,0:T(8,128)}, f32[128,128]{1,0:T(8,128)}) custom-call(f32[1]{0:T(128)S(6)} %copy.10.ls_ref, f32[1]{0:T(128)S(6)} %copy.11.lb_ref, bf16[128,1536]{1,0:T(8,128)(2,1)} %imgf_ref.1, bf16[128,4096]{1,0:T(8,128)(2,1)} %txtf_ref.1, bf16[1536,1024]{1,0:T(8,128)(2,1)} %imgh_ref.1, ...), custom_call_target="tpu_custom_call" | custom-call | flops 5000000000 | bytes 14000000 | tf_op jit(solution)/shard_map/contrastive/pallas_call | solution.py:469
  69.8 2.0 %finish.1 = (f32[1]{0:T(128)}, f32[2]{0:T(128)}, f32[6,1024]{1,0:T(8,128)}, f32[128,1024]{1,0:T(8,128)}) custom-call(f32[1]{0:T(128)S(6)} %copy.10.ls_ref, f32[8,256]{1,0:T(8,128)} %get-tuple-element.12.st_ref, f32[6,1024]{1,0:T(8,128)} %get-tuple-element.13.hgs_ref, f32[128,1024]{1,0:T(8,128)} %get-tuple-element.14.tgs_ref, ...), custom_call_target="tpu_custom_call" | custom-call | tf_op jit(solution)/shard_map/finish/pallas_call | solution.py:524

commit v8 on v7

--- a/solution.py
+++ b/solution.py
@@ -314,9 +314,10 @@
     text_group(5)
     sums_send(TXT, acc_i, rcv_i)
 
-    for n in range(3):
-        stat[n : n + 1, :] = totals[n]
-    stat[3:8, :] = jnp.zeros((5, B), jnp.float32)
+    stat[...] = jnp.zeros((8, 2 * B), jnp.float32)
+    stat[0:1, 0:B] = totals[0]
+    stat[0:1, B : 2 * B] = totals[1]
+    stat[1:2, 0:B] = totals[2]
     send(SIB + 2, stat, stats2, sib)
     unit = unit_i[...]
     dunit = sums(TXT, acc_i, rcv_i)
@@ -372,14 +373,14 @@
             span = pl.ds(pl.multiple_of(n * 384 + i * 48, 16), 48)
             value = part[span, :] + part_rcv[span, :]
             to_y, to_x = 2 * n + i // 4, i % 4
-            out_a[to_x, pl.ds(pl.multiple_of(to_y * 48, 16), 48), :] = value[:, :B]
-            out_b[to_y, 48 * to_x : 48 * to_x + 48, :] = value[:, B:]
+            out_a[to_x, pl.ds(pl.multiple_of(to_y * 32, 32), 32), :] = value[:32, :]
+            out_b[to_y, 16 * to_x : 16 * to_x + 16, :] = value[32:, :]
         for i in range(2):
             to_y = 2 * n + i
             o = lax.rem(to_y - y + 4, 4)
             send_if(to_y != y, PLB + o, out_b.at[to_y], in_b.at[o], y_mate(o))
     for n in range(4):
-        out_a[n, 192:200, :] = both
+        out_a[n, 128:136, :] = both
     for o in (1, 2, 3):
         send(PLA + o, out_a.at[lax.rem(x + o, 4)], in_a.at[o], x_mate(o))
 
@@ -396,24 +397,21 @@
 
     total = summed(PLB, out_b, y, in_b)
     for n in range(4):
-        out_b2[n] = total[48 * n : 48 * n + 48, :]
+        out_b2[n] = total[16 * n : 16 * n + 16, :]
     for o in (1, 2, 3):
         send(PLB + 4 + o, out_b2.at[lax.rem(x + o, 4)], in_b2.at[o], x_mate(o))
     total = summed(PLA, out_a, x, in_a)
     for n in range(4):
-        out_a2[n, 0:48, :] = total[48 * n : 48 * n + 48, :]
-        out_a2[n, 48:56, :] = total[192:200, :]
+        out_a2[n, 0:32, :] = total[32 * n : 32 * n + 32, :]
+        out_a2[n, 32:40, :] = total[128:136, :]
     for o in (1, 2, 3):
         send(PLA + 4 + o, out_a2.at[lax.rem(y + o, 4)], in_a2.at[o], y_mate(o))
     total_b = summed(PLB + 4, out_b2, x, in_b2)
     total_a = summed(PLA + 4, out_a2, y, in_a2)
+    total = jnp.concatenate([total_a[:32, :], total_b], axis=0)
     for j in range(8):
-        tails[j, 0:6, 0:B] = total_a[6 * j : 6 * j + 6, :]
-        tails[j, 0:6, B : 2 * B] = total_b[6 * j : 6 * j + 6, :]
-        tails[j, 6:7, 0:B] = total_a[48:49, :]
-        tails[j, 6:7, B : 2 * B] = total_a[49:50, :]
-        tails[j, 7:8, 0:B] = total_a[50:51, :]
-        tails[j, 7:8, B : 2 * B] = jnp.zeros((1, B), jnp.float32)
+        tails[j, 0:6, :] = total[6 * j : 6 * j + 6, :]
+        tails[j, 6:8, :] = total_a[32:34, :]
     for j in range(8):
         @pl.when(first_owner + j != me)
         def _():
@@ -496,21 +494,21 @@
             pltpu.VMEM((B, E), f32),
             pltpu.VMEM((4, 256, B), bf16),
             pltpu.VMEM((256, 4 * B), bf16),
-            pltpu.VMEM((8, 128), f32),
-            pltpu.VMEM((8, 128), f32),
+            pltpu.VMEM((8, 256), f32),
+            pltpu.VMEM((8, 256), f32),
             pltpu.VMEM((8, 8, 256), f32),
             pltpu.VMEM((768, 256), f32),
             pltpu.VMEM((768, 256), f32),
             pltpu.VMEM((768, 256), f32),
             pltpu.VMEM((8, 8, 256), f32),
-            pltpu.VMEM((4, 200, 128), f32),
-            pltpu.VMEM((4, 200, 128), f32),
-            pltpu.VMEM((4, 192, 128), f32),
-            pltpu.VMEM((4, 192, 128), f32),
-            pltpu.VMEM((4, 56, 128), f32),
-            pltpu.VMEM((4, 56, 128), f32),
-            pltpu.VMEM((4, 48, 128), f32),
-            pltpu.VMEM((4, 48, 128), f32),
+            pltpu.VMEM((4, 136, 256), f32),
+            pltpu.VMEM((4, 136, 256), f32),
+            pltpu.VMEM((4, 64, 256), f32),
+            pltpu.VMEM((4, 64, 256), f32),
+            pltpu.VMEM((4, 40, 256), f32),
+            pltpu.VMEM((4, 40, 256), f32),
+            pltpu.VMEM((4, 16, 256), f32),
+            pltpu.VMEM((4, 16, 256), f32),
             pltpu.SemaphoreType.DMA((16,)),
             pltpu.SemaphoreType.DMA((IDS,)),
             pltpu.SemaphoreType.DMA((IDS,)),

time: 72.1 us -> 71.3 us (0.989)
  Pallas kernels: 69.9 us -> 68.8 us
    pallas_call x1, Pallas kernels: 67.8 us -> 66.8 us  [shards(): pl.pallas_call(kernel, out_shape=(jax.ShapeDtypeStruct((8, 2 * B), f32),...]
where the time goes in v8:
time: 71.3 us; the launch traced here: 70.7 us
  Pallas kernels  68.8 us (96%)
  between operations  1.93 us (3%)
    pallas_call x1, Pallas kernels, shards(): pl.pallas_call(kernel, out_shape=(jax.ShapeDtypeStruct((8, 2 * B), f32),...  66.8 us
    pallas_call x1, Pallas kernels, shards(): pl.pallas_call(finish, out_shape=(jax.ShapeDtypeStruct((1,), f32), jax.Sh...  2.02 us

profile of v8, /device:TPU:1, one launch (start us, length us, event | category | flops | bytes accessed | tf_op | source)
XLA Modules:
  0.0 70.7 jit_solution(12813557104611233572)
XLA Ops:
  1.9 66.8 %contrastive.1 = (f32[8,256]{1,0:T(8,128)}, f32[6,1024]{1,0:T(8,128)}, f32[128,1024]{1,0:T(8,128)}, f32[128,128]{1,0:T(8,128)}) custom-call(f32[1]{0:T(128)S(6)} %copy.10.ls_ref, f32[1]{0:T(128)S(6)} %copy.11.lb_ref, bf16[128,1536]{1,0:T(8,128)(2,1)} %imgf_ref.1, bf16[128,4096]{1,0:T(8,128)(2,1)} %txtf_ref.1, bf16[1536,1024]{1,0:T(8,128)(2,1)} %imgh_ref.1, ...), custom_call_target="tpu_custom_call" | custom-call | flops 5000000000 | bytes 14000000 | tf_op jit(solution)/shard_map/contrastive/pallas_call | solution.py:467
  68.7 2.0 %finish.1 = (f32[1]{0:T(128)}, f32[2]{0:T(128)}, f32[6,1024]{1,0:T(8,128)}, f32[128,1024]{1,0:T(8,128)}) custom-call(f32[1]{0:T(128)S(6)} %copy.10.ls_ref, f32[8,256]{1,0:T(8,128)} %get-tuple-element.12.st_ref, f32[6,1024]{1,0:T(8,128)} %get-tuple-element.13.hgs_ref, f32[128,1024]{1,0:T(8,128)} %get-tuple-element.14.tgs_ref, ...), custom_call_target="tpu_custom_call" | custom-call | tf_op jit(solution)/shard_map/finish/pallas_call | solution.py:522

commit v9 on v8

--- a/solution.py
+++ b/solution.py
@@ -15,14 +15,15 @@
 CH = 512
 
 TXT = 0
-IMG = 24
-FEA = 48
-DLO = 52
-SIB = 56
+IMG = 26
+FEA = 52
+DLO = 56
+SIB = 100
 PLA = 60
 PLB = 68
 OWN = 76
-IDS = 84
+IDS = 104
+PIECES = ((0, 32), (32, 48), (80, 48))
 
 
 def kernel(
@@ -146,73 +147,73 @@
     def crossed(at, q):
         return q - 4 * (at + q < 4).astype(jnp.int32)
 
-    def slot(ref, off, half=None):
-        if half is None:
+    def slot(ref, off, piece=None):
+        if piece is None:
             return ref.at[2 * (3 + off) + core]
-        return ref.at[2 * (3 + off) + core, pl.ds(half * (B // 2), B // 2)]
-
-    def row_send(base, ref, half):
-        send(base + 4 + (half or 0), slot(ref, 0, half), slot(ref, in_row(right_x, 3), half), right)
-        send(base + (half or 0), slot(ref, 0, half), slot(ref, in_row(left_x, 1), half), left)
-
-    def row_wait(base, ref, q, half):
-        arrived(base + 2 * (q - 1) + (half or 0), slot(ref, in_row(x, q), half))
+        return ref.at[2 * (3 + off) + core, pl.ds(*PIECES[piece])]
+
+    def row_send(base, ref, piece):
+        send(base + 6 + (piece or 0), slot(ref, 0, piece), slot(ref, in_row(right_x, 3), piece), right)
+        send(base + (piece or 0), slot(ref, 0, piece), slot(ref, in_row(left_x, 1), piece), left)
+
+    def row_wait(base, ref, q, piece):
+        arrived(base + 3 * (q - 1) + (piece or 0), slot(ref, in_row(x, q), piece))
 
     right_on = (x == 3) | ((core == 0) & (x < 2))
     left_on = (x == 0) | ((core == 1) & (x >= 2))
 
-    def opposite_send(base, ref, half):
-        i = base + 2 + (half or 0)
-        send_if(right_on, i, slot(ref, in_row(x, 3), half), slot(ref, in_row(right_x, 2), half), right)
+    def opposite_send(base, ref, piece):
+        i = base + 3 + (piece or 0)
+        send_if(right_on, i, slot(ref, in_row(x, 3), piece), slot(ref, in_row(right_x, 2), piece), right)
         send_if(
-            left_on, base + 21 + (half or 0), slot(ref, in_row(x, 1), half), slot(ref, in_row(left_x, 2), half),
+            left_on, base + 21 + (piece or 0), slot(ref, in_row(x, 1), piece), slot(ref, in_row(left_x, 2), piece),
             left, i,
         )
 
-    def cross_send(base, ref, q, half):
+    def cross_send(base, ref, q, piece):
         dev = jnp.where(x + q < 4, up, down)
-        i = base + 6 + 2 * (q - 1) + (half or 0)
-        src, dst = slot(ref, in_row(x, q), half), slot(ref, crossed(x, q), half)
+        i = base + 9 + 3 * (q - 1) + (piece or 0)
+        src, dst = slot(ref, in_row(x, q), piece), slot(ref, crossed(x, q), piece)
         if q == 2:
             send_if(inner, i, src, dst, dev)
         else:
             send(i, src, dst, dev)
 
-    def cross_wait(base, ref, q, half):
-        arrived(base + 6 + 2 * (q - 1) + (half or 0), slot(ref, crossed(x, q), half))
-
-    def cross_wait_rest(base, ref, q, half):
+    def cross_wait(base, ref, q, piece):
+        arrived(base + 9 + 3 * (q - 1) + (piece or 0), slot(ref, crossed(x, q), piece))
+
+    def cross_wait_rest(base, ref, q, piece):
         @pl.when(x != (q + 1) // 2)
         def _():
-            cross_wait(base, ref, q, half)
-
-    def hand_on(base, ref, half):
+            cross_wait(base, ref, q, piece)
+
+    def hand_on(base, ref, piece):
         for at in (1, 2):
             @pl.when(x == at)
             def _():
-                cross_wait(base, ref, 2 * at - 1, half)
+                cross_wait(base, ref, 2 * at - 1, piece)
         near = jnp.where(inner, x, 1)
         taken = crossed(near, 2 * near - 1)
         to = 3 * (near - 1)
         send_if(
-            inner, base + 12 + (half or 0), slot(ref, taken, half), slot(ref, crossed(to, 2), half),
-            row_first + 2 * to, base + 8 + (half or 0),
+            inner, base + 18 + (piece or 0), slot(ref, taken, piece), slot(ref, crossed(to, 2), piece),
+            row_first + 2 * to, base + 12 + (piece or 0),
         )
 
     def own_rows(ref, of):
         return ref.at[pl.ds(pl.multiple_of(of * B, B), B)]
 
     def own_send(base, ref):
-        send(base + 14, slot(ref, 0), slot(ref, 0), sib)
+        send(base + 24, slot(ref, 0), slot(ref, 0), sib)
 
     def own_wait(base, ref):
-        arrived(base + 14, ref.at[7 - core])
+        arrived(base + 24, ref.at[7 - core])
 
     def sums_send(base, acc, rcv):
-        send(base + 15, own_rows(acc, 1 - core), rcv, sib)
+        send(base + 25, own_rows(acc, 1 - core), rcv, sib)
 
     def sums(base, acc, rcv):
-        arrived(base + 15, rcv)
+        arrived(base + 25, rcv)
         return own_rows(acc, core)[...] + rcv[...]
 
     def project(read, head, acc, first, count):
@@ -233,8 +234,8 @@
     project(lambda j: txtf[:, pl.ds(j * CH, CH)], txth, sum_t, 2, DT // CH)
     normalize(sum_t, unit_t, inv_t, texts)
     pl.semaphore_wait(barrier, 12 + 8 - owner_is_me.astype(jnp.int32))
-    for half in (0, 1):
-        row_send(TXT, texts, half)
+    for piece in range(len(PIECES)):
+        row_send(TXT, texts, piece)
     own_send(TXT, texts)
     loads[0].wait()
     send(FEA + 1, fea(0), fea(1), z_mate(-side))
@@ -291,26 +292,26 @@
 
     own_wait(IMG, images)
     text_group(0)
-    for half in (0, 1):
+    for piece in range(len(PIECES)):
         for q in (1, 3):
-            row_wait(TXT, texts, q, half)
-            cross_send(TXT, texts, q, half)
-        opposite_send(TXT, texts, half)
-    for half in (0, 1):
-        row_wait(TXT, texts, 2, half)
-        cross_send(TXT, texts, 2, half)
-        hand_on(TXT, texts, half)
+            row_wait(TXT, texts, q, piece)
+            cross_send(TXT, texts, q, piece)
+        opposite_send(TXT, texts, piece)
+    for piece in range(len(PIECES)):
+        row_wait(TXT, texts, 2, piece)
+        cross_send(TXT, texts, 2, piece)
+        hand_on(TXT, texts, piece)
     row_send(IMG, images, None)
     arrived(FEA + 1, fea(1))
     send(FEA + 2, fea(1), fea(2), z_mate(-side))
     text_group(1, 3)
     text_group(2)
     for q in (1, 3):
-        for half in (0, 1):
-            cross_wait_rest(TXT, texts, q, half)
+        for piece in range(len(PIECES)):
+            cross_wait_rest(TXT, texts, q, piece)
     text_group(4, 6)
-    for half in (0, 1):
-        cross_wait(TXT, texts, 2, half)
+    for piece in range(len(PIECES)):
+        cross_wait(TXT, texts, 2, piece)
     text_group(5)
     sums_send(TXT, acc_i, rcv_i)
 
@@ -354,8 +355,8 @@
     def part_rows(ref, n):
         return ref.at[pl.ds(pl.multiple_of(n * 384, 384), 384)]
 
-    def product(half, n, ref):
-        columns = pl.ds(pl.multiple_of(half * 768 + n * 384, 128), 384)
+    def product(piece, n, ref):
+        columns = pl.ds(pl.multiple_of(piece * 768 + n * 384, 128), 384)
         part_rows(ref, n)[...] = jnp.dot(
             dgat[...], feats[:, columns], preferred_element_type=jnp.float32
         ).T

time: 71.3 us -> 71.5 us (level)
  no operation moved by 1% of the time
where the time goes in v9:
time: 71.5 us; the launch traced here: 70.9 us
  Pallas kernels  69 us (97%)
  between operations  1.93 us (3%)
    pallas_call x1, Pallas kernels, shards(): pl.pallas_call(kernel, out_shape=(jax.ShapeDtypeStruct((8, 2 * B), f32),...  67 us
    pallas_call x1, Pallas kernels, shards(): pl.pallas_call(finish, out_shape=(jax.ShapeDtypeStruct((1,), f32), jax.Sh...  2.02 us

profile of v9, /device:TPU:1, one launch (start us, length us, event | category | flops | bytes accessed | tf_op | source)
XLA Modules:
  0.0 70.9 jit_solution(3361115323722390803)
XLA Ops:
  1.9 67.0 %contrastive.1 = (f32[8,256]{1,0:T(8,128)}, f32[6,1024]{1,0:T(8,128)}, f32[128,1024]{1,0:T(8,128)}, f32[128,128]{1,0:T(8,128)}) custom-call(f32[1]{0:T(128)S(6)} %copy.10.ls_ref, f32[1]{0:T(128)S(6)} %copy.11.lb_ref, bf16[128,1536]{1,0:T(8,128)(2,1)} %imgf_ref.1, bf16[128,4096]{1,0:T(8,128)(2,1)} %txtf_ref.1, bf16[1536,1024]{1,0:T(8,128)(2,1)} %imgh_ref.1, ...), custom_call_target="tpu_custom_call" | custom-call | flops 5000000000 | bytes 14000000 | tf_op jit(solution)/shard_map/contrastive/pallas_call | solution.py:468
  68.9 2.0 %finish.1 = (f32[1]{0:T(128)}, f32[2]{0:T(128)}, f32[6,1024]{1,0:T(8,128)}, f32[128,1024]{1,0:T(8,128)}) custom-call(f32[1]{0:T(128)S(6)} %copy.10.ls_ref, f32[8,256]{1,0:T(8,128)} %get-tuple-element.12.st_ref, f32[6,1024]{1,0:T(8,128)} %get-tuple-element.13.hgs_ref, f32[128,1024]{1,0:T(8,128)} %get-tuple-element.14.tgs_ref, ...), custom_call_target="tpu_custom_call" | custom-call | tf_op jit(solution)/shard_map/finish/pallas_call | solution.py:523

commit v10 on v8

--- a/solution.py
+++ b/solution.py
@@ -344,7 +344,6 @@
     opposite_send(IMG, images, None)
     own_wait(TXT, texts)
     image_group(0)
-    image_group(1, 3)
 
     for n in (1, 2, 3):
         arrived(DLO + n, window(n))
@@ -387,6 +386,7 @@
     row_wait(IMG, images, 2, None)
     cross_send(IMG, images, 2, None)
     hand_on(IMG, images, None)
+    image_group(1, 3)
     image_group(2)
     drain(early, early_if)
 
@@ -406,6 +406,9 @@
         out_a2[n, 32:40, :] = total[128:136, :]
     for o in (1, 2, 3):
         send(PLA + 4 + o, out_a2.at[lax.rem(y + o, 4)], in_a2.at[o], y_mate(o))
+    for q in (1, 3):
+        cross_wait_rest(IMG, images, q, None)
+    image_group(4, 6)
     total_b = summed(PLB + 4, out_b2, x, in_b2)
     total_a = summed(PLA + 4, out_a2, y, in_a2)
     total = jnp.concatenate([total_a[:32, :], total_b], axis=0)
@@ -425,9 +428,6 @@
         def _():
             owned[z] = tails[j]
 
-    for q in (1, 3):
-        cross_wait_rest(IMG, images, q, None)
-    image_group(4, 6)
     cross_wait(IMG, images, 2, None)
     image_group(5)
     sums_send(IMG, acc_t, rcv_t)

time: 71.3 us -> 71.3 us (level)
  no operation moved by 1% of the time
where the time goes in v10:
time: 71.3 us; the launch traced here: 70.7 us
  Pallas kernels  68.8 us (96%)
  between operations  1.93 us (3%)
    pallas_call x1, Pallas kernels, shards(): pl.pallas_call(kernel, out_shape=(jax.ShapeDtypeStruct((8, 2 * B), f32),...  66.8 us
    pallas_call x1, Pallas kernels, shards(): pl.pallas_call(finish, out_shape=(jax.ShapeDtypeStruct((1,), f32), jax.Sh...  2.02 us

profile of v10, /device:TPU:1, one launch (start us, length us, event | category | flops | bytes accessed | tf_op | source)
XLA Modules:
  0.0 70.7 jit_solution(17001653482315028131)
XLA Ops:
  1.9 66.8 %contrastive.1 = (f32[8,256]{1,0:T(8,128)}, f32[6,1024]{1,0:T(8,128)}, f32[128,1024]{1,0:T(8,128)}, f32[128,128]{1,0:T(8,128)}) custom-call(f32[1]{0:T(128)S(6)} %copy.10.ls_ref, f32[1]{0:T(128)S(6)} %copy.11.lb_ref, bf16[128,1536]{1,0:T(8,128)(2,1)} %imgf_ref.1, bf16[128,4096]{1,0:T(8,128)(2,1)} %txtf_ref.1, bf16[1536,1024]{1,0:T(8,128)(2,1)} %imgh_ref.1, ...), custom_call_target="tpu_custom_call" | custom-call | flops 5000000000 | bytes 14000000 | tf_op jit(solution)/shard_map/contrastive/pallas_call | solution.py:467
  68.7 2.0 %finish.1 = (f32[1]{0:T(128)}, f32[2]{0:T(128)}, f32[6,1024]{1,0:T(8,128)}, f32[128,1024]{1,0:T(8,128)}) custom-call(f32[1]{0:T(128)S(6)} %copy.10.ls_ref, f32[8,256]{1,0:T(8,128)} %get-tuple-element.12.st_ref, f32[6,1024]{1,0:T(8,128)} %get-tuple-element.13.hgs_ref, f32[128,1024]{1,0:T(8,128)} %get-tuple-element.14.tgs_ref, ...), custom_call_target="tpu_custom_call" | custom-call | tf_op jit(solution)/shard_map/finish/pallas_call | solution.py:522

commit v11 on v10

--- a/solution.py
+++ b/solution.py
@@ -313,6 +313,26 @@
         cross_wait(TXT, texts, 2, half)
     text_group(5)
     sums_send(TXT, acc_i, rcv_i)
+    early, early_if = list(sent), list(sent_if)
+    sent.clear()
+    sent_if.clear()
+
+    def image_forward(late):
+        for q, at, on, i, to, to_q, dev in (
+            (1, 0, left_on, IMG + 21, left_x, 2, left), (3, 3, right_on, IMG + 2, right_x, 2, right)
+        ):
+            now = (x == at) if late else (x != at)
+
+            @pl.when(now)
+            def _():
+                row_wait(IMG, images, q, None)
+
+            src = slot(images, in_row(x, q))
+            i_cross = IMG + 6 + 2 * (q - 1)
+            send_if(now, i_cross, src, slot(images, crossed(x, q)), jnp.where(x + q < 4, up, down))
+            send_if(now & on, i, src, slot(images, in_row(to, to_q)), dev, IMG + 2)
+
+    image_forward(False)
 
     stat[...] = jnp.zeros((8, 2 * B), jnp.float32)
     stat[0:1, 0:B] = totals[0]
@@ -335,13 +355,7 @@
         else:
             dlow_t[n] = turned
             send(DLO + n, dlow_t.at[n], window(n), z_mate(off))
-    early, early_if = list(sent), list(sent_if)
-    sent.clear()
-    sent_if.clear()
-    for q in (1, 3):
-        row_wait(IMG, images, q, None)
-        cross_send(IMG, images, q, None)
-    opposite_send(IMG, images, None)
+    image_forward(True)
     own_wait(TXT, texts)
     image_group(0)
 

time: 71.3 us -> 75.3 us (1.056)
  Pallas kernels: 68.8 us -> 72.7 us
    pallas_call x1, Pallas kernels: 66.8 us -> 70.7 us  [shards(): pl.pallas_call(kernel, out_shape=(jax.ShapeDtypeStruct((8, 2 * B), f32),...]
where the time goes in v11:
time: 75.3 us; the launch traced here: 74.6 us
  Pallas kernels  72.7 us (97%)
  between operations  1.93 us (3%)
    pallas_call x1, Pallas kernels, shards(): pl.pallas_call(kernel, out_shape=(jax.ShapeDtypeStruct((8, 2 * B), f32),...  70.7 us
    pallas_call x1, Pallas kernels, shards(): pl.pallas_call(finish, out_shape=(jax.ShapeDtypeStruct((1,), f32), jax.Sh...  2.02 us

profile of v11, /device:TPU:1, one launch (start us, length us, event | category | flops | bytes accessed | tf_op | source)
XLA Modules:
  0.0 74.6 jit_solution(15108848846111959256)
XLA Ops:
  1.9 70.7 %contrastive.1 = (f32[8,256]{1,0:T(8,128)}, f32[6,1024]{1,0:T(8,128)}, f32[128,1024]{1,0:T(8,128)}, f32[128,128]{1,0:T(8,128)}) custom-call(f32[1]{0:T(128)S(6)} %copy.10.ls_ref, f32[1]{0:T(128)S(6)} %copy.11.lb_ref, bf16[128,1536]{1,0:T(8,128)(2,1)} %imgf_ref.1, bf16[128,4096]{1,0:T(8,128)(2,1)} %txtf_ref.1, bf16[1536,1024]{1,0:T(8,128)(2,1)} %imgh_ref.1, ...), custom_call_target="tpu_custom_call" | custom-call | flops 5000000000 | bytes 14000000 | tf_op jit(solution)/shard_map/contrastive/pallas_call | solution.py:481
  72.6 2.0 %finish.1 = (f32[1]{0:T(128)}, f32[2]{0:T(128)}, f32[6,1024]{1,0:T(8,128)}, f32[128,1024]{1,0:T(8,128)}) custom-call(f32[1]{0:T(128)S(6)} %copy.10.ls_ref, f32[8,256]{1,0:T(8,128)} %get-tuple-element.12.st_ref, f32[6,1024]{1,0:T(8,128)} %get-tuple-element.13.hgs_ref, f32[128,1024]{1,0:T(8,128)} %get-tuple-element.14.tgs_ref, ...), custom_call_target="tpu_custom_call" | custom-call | tf_op jit(solution)/shard_map/finish/pallas_call | solution.py:536

commit v12 on v10

--- a/solution.py
+++ b/solution.py
@@ -300,7 +300,6 @@
         row_wait(TXT, texts, 2, half)
         cross_send(TXT, texts, 2, half)
         hand_on(TXT, texts, half)
-    row_send(IMG, images, None)
     arrived(FEA + 1, fea(1))
     send(FEA + 2, fea(1), fea(2), z_mate(-side))
     text_group(1, 3)
@@ -308,6 +307,7 @@
     for q in (1, 3):
         for half in (0, 1):
             cross_wait_rest(TXT, texts, q, half)
+    row_send(IMG, images, None)
     text_group(4, 6)
     for half in (0, 1):
         cross_wait(TXT, texts, 2, half)

time: 71.3 us -> 71.9 us (level)
  Pallas kernels: 68.8 us -> 69.8 us
    pallas_call x1, Pallas kernels: 66.8 us -> 67.8 us  [shards(): pl.pallas_call(kernel, out_shape=(jax.ShapeDtypeStruct((8, 2 * B), f32),...]
where the time goes in v12:
time: 71.9 us; the launch traced here: 71.7 us
  Pallas kernels  69.8 us (97%)
  between operations  1.93 us (3%)
    pallas_call x1, Pallas kernels, shards(): pl.pallas_call(kernel, out_shape=(jax.ShapeDtypeStruct((8, 2 * B), f32),...  67.8 us
    pallas_call x1, Pallas kernels, shards(): pl.pallas_call(finish, out_shape=(jax.ShapeDtypeStruct((1,), f32), jax.Sh...  2.02 us

profile of v12, /device:TPU:1, one launch (start us, length us, event | category | flops | bytes accessed | tf_op | source)
XLA Modules:
  0.0 71.7 jit_solution(2097141216679474342)
XLA Ops:
  1.9 67.8 %contrastive.1 = (f32[8,256]{1,0:T(8,128)}, f32[6,1024]{1,0:T(8,128)}, f32[128,1024]{1,0:T(8,128)}, f32[128,128]{1,0:T(8,128)}) custom-call(f32[1]{0:T(128)S(6)} %copy.10.ls_ref, f32[1]{0:T(128)S(6)} %copy.11.lb_ref, bf16[128,1536]{1,0:T(8,128)(2,1)} %imgf_ref.1, bf16[128,4096]{1,0:T(8,128)(2,1)} %txtf_ref.1, bf16[1536,1024]{1,0:T(8,128)(2,1)} %imgh_ref.1, ...), custom_call_target="tpu_custom_call" | custom-call | flops 5000000000 | bytes 14000000 | tf_op jit(solution)/shard_map/contrastive/pallas_call | solution.py:467
  69.7 2.0 %finish.1 = (f32[1]{0:T(128)}, f32[2]{0:T(128)}, f32[6,1024]{1,0:T(8,128)}, f32[128,1024]{1,0:T(8,128)}) custom-call(f32[1]{0:T(128)S(6)} %copy.10.ls_ref, f32[8,256]{1,0:T(8,128)} %get-tuple-element.12.st_ref, f32[6,1024]{1,0:T(8,128)} %get-tuple-element.13.hgs_ref, f32[128,1024]{1,0:T(8,128)} %get-tuple-element.14.tgs_ref, ...), custom_call_target="tpu_custom_call" | custom-call | tf_op jit(solution)/shard_map/finish/pallas_call | solution.py:522

commit v13 on v10

--- a/solution.py
+++ b/solution.py
@@ -30,7 +30,7 @@
     st_ref, hg_ref, tg_ref, tinv_ref,
     txtf, imgh, txth, feats, texts, images, unit_t, unit_i, acc_t, acc_i, inv_t, inv_i,
     sum_t, sum_i, rcv_t, rcv_i, dlow, dlow_t, dgat, stat, stats2, tails, part_sib, part_rcv, part, owned,
-    out_a, in_a, out_b, in_b, out_a2, in_a2, out_b2, in_b2,
+    out_a, in_a, ring_a, out_b, in_b, out_a2, in_a2, out_b2, in_b2,
     load_sem, send_sem, recv_sem,
 ):
     me = lax.axis_index("dp")
@@ -59,7 +59,7 @@
     y = spot // 4
 
     def x_mate(off):
-        return row_first + 2 * lax.rem(x + off, 4)
+        return row_first + 2 * lax.rem(x + off + 4, 4)
 
     def y_mate(off):
         return 32 * z + 8 * lax.rem(y + off, 4) + 2 * x + core
@@ -380,13 +380,16 @@
             send_if(to_y != y, PLB + o, out_b.at[to_y], in_b.at[o], y_mate(o))
     for n in range(4):
         out_a[n, 128:136, :] = both
-    for o in (1, 2, 3):
-        send(PLA + o, out_a.at[lax.rem(x + o, 4)], in_a.at[o], x_mate(o))
+    send(PLA + 1, out_a.at[lax.rem(x + 2, 4)], in_a.at[1], x_mate(side))
+    send(PLA + 2, out_a.at[lax.rem(x - side + 4, 4)], in_a.at[2], x_mate(-side))
 
     row_wait(IMG, images, 2, None)
     cross_send(IMG, images, 2, None)
     hand_on(IMG, images, None)
     image_group(1, 3)
+    arrived(PLA + 1, in_a.at[1])
+    ring_a[...] = out_a[lax.rem(x + side + 4, 4)] + in_a[1]
+    send(PLA + 3, ring_a, in_a.at[3], x_mate(side))
     image_group(2)
     drain(early, early_if)
 
@@ -400,7 +403,9 @@
         out_b2[n] = total[16 * n : 16 * n + 16, :]
     for o in (1, 2, 3):
         send(PLB + 4 + o, out_b2.at[lax.rem(x + o, 4)], in_b2.at[o], x_mate(o))
-    total = summed(PLA, out_a, x, in_a)
+    arrived(PLA + 2, in_a.at[2])
+    arrived(PLA + 3, in_a.at[3])
+    total = out_a[x] + in_a[2] + in_a[3]
     for n in range(4):
         out_a2[n, 0:32, :] = total[32 * n : 32 * n + 32, :]
         out_a2[n, 32:40, :] = total[128:136, :]
@@ -503,6 +508,7 @@
             pltpu.VMEM((8, 8, 256), f32),
             pltpu.VMEM((4, 136, 256), f32),
             pltpu.VMEM((4, 136, 256), f32),
+            pltpu.VMEM((136, 256), f32),
             pltpu.VMEM((4, 64, 256), f32),
             pltpu.VMEM((4, 64, 256), f32),
             pltpu.VMEM((4, 40, 256), f32),

time: 71.3 us -> 71.7 us (level)
  no operation moved by 1% of the time
where the time goes in v13:
time: 71.7 us; the launch traced here: 70.6 us
  Pallas kernels  68.7 us (96%)
  between operations  1.93 us (3%)
    pallas_call x1, Pallas kernels, shards(): pl.pallas_call(kernel, out_shape=(jax.ShapeDtypeStruct((8, 2 * B), f32),...  66.7 us
    pallas_call x1, Pallas kernels, shards(): pl.pallas_call(finish, out_shape=(jax.ShapeDtypeStruct((1,), f32), jax.Sh...  2.02 us

profile of v13, /device:TPU:1, one launch (start us, length us, event | category | flops | bytes accessed | tf_op | source)
XLA Modules:
  0.0 70.6 jit_solution(16772765906695936538)
XLA Ops:
  1.9 66.7 %contrastive.1 = (f32[8,256]{1,0:T(8,128)}, f32[6,1024]{1,0:T(8,128)}, f32[128,1024]{1,0:T(8,128)}, f32[128,128]{1,0:T(8,128)}) custom-call(f32[1]{0:T(128)S(6)} %copy.10.ls_ref, f32[1]{0:T(128)S(6)} %copy.11.lb_ref, bf16[128,1536]{1,0:T(8,128)(2,1)} %imgf_ref.1, bf16[128,4096]{1,0:T(8,128)(2,1)} %txtf_ref.1, bf16[1536,1024]{1,0:T(8,128)(2,1)} %imgh_ref.1, ...), custom_call_target="tpu_custom_call" | custom-call | flops 5000000000 | bytes 14000000 | tf_op jit(solution)/shard_map/contrastive/pallas_call | solution.py:472
  68.6 2.0 %finish.1 = (f32[1]{0:T(128)}, f32[2]{0:T(128)}, f32[6,1024]{1,0:T(8,128)}, f32[128,1024]{1,0:T(8,128)}) custom-call(f32[1]{0:T(128)S(6)} %copy.10.ls_ref, f32[8,256]{1,0:T(8,128)} %get-tuple-element.12.st_ref, f32[6,1024]{1,0:T(8,128)} %get-tuple-element.13.hgs_ref, f32[128,1024]{1,0:T(8,128)} %get-tuple-element.14.tgs_ref, ...), custom_call_target="tpu_custom_call" | custom-call | tf_op jit(solution)/shard_map/finish/pallas_call | solution.py:528

commit v14 on v13

--- a/solution.py
+++ b/solution.py
@@ -20,7 +20,6 @@
 DLO = 52
 SIB = 56
 PLA = 60
-PLB = 68
 OWN = 76
 IDS = 84
 
@@ -30,7 +29,7 @@
     st_ref, hg_ref, tg_ref, tinv_ref,
     txtf, imgh, txth, feats, texts, images, unit_t, unit_i, acc_t, acc_i, inv_t, inv_i,
     sum_t, sum_i, rcv_t, rcv_i, dlow, dlow_t, dgat, stat, stats2, tails, part_sib, part_rcv, part, owned,
-    out_a, in_a, ring_a, out_b, in_b, out_a2, in_a2, out_b2, in_b2,
+    out_a, in_a, ring_a, out_a2, in_a2,
     load_sem, send_sem, recv_sem,
 ):
     me = lax.axis_index("dp")
@@ -372,24 +371,19 @@
             span = pl.ds(pl.multiple_of(n * 384 + i * 48, 16), 48)
             value = part[span, :] + part_rcv[span, :]
             to_y, to_x = 2 * n + i // 4, i % 4
-            out_a[to_x, pl.ds(pl.multiple_of(to_y * 32, 32), 32), :] = value[:32, :]
-            out_b[to_y, 16 * to_x : 16 * to_x + 16, :] = value[32:, :]
-        for i in range(2):
-            to_y = 2 * n + i
-            o = lax.rem(to_y - y + 4, 4)
-            send_if(to_y != y, PLB + o, out_b.at[to_y], in_b.at[o], y_mate(o))
+            out_a[to_x, pl.ds(pl.multiple_of(to_y * 48, 16), 48), :] = value
     for n in range(4):
-        out_a[n, 128:136, :] = both
+        out_a[n, 192:200, :] = both
     send(PLA + 1, out_a.at[lax.rem(x + 2, 4)], in_a.at[1], x_mate(side))
     send(PLA + 2, out_a.at[lax.rem(x - side + 4, 4)], in_a.at[2], x_mate(-side))
 
     row_wait(IMG, images, 2, None)
     cross_send(IMG, images, 2, None)
-    hand_on(IMG, images, None)
     image_group(1, 3)
     arrived(PLA + 1, in_a.at[1])
     ring_a[...] = out_a[lax.rem(x + side + 4, 4)] + in_a[1]
     send(PLA + 3, ring_a, in_a.at[3], x_mate(side))
+    hand_on(IMG, images, None)
     image_group(2)
     drain(early, early_if)
 
@@ -398,28 +392,21 @@
             arrived(base + o, got.at[o])
         return out[at] + got[1] + got[2] + got[3]
 
-    total = summed(PLB, out_b, y, in_b)
-    for n in range(4):
-        out_b2[n] = total[16 * n : 16 * n + 16, :]
-    for o in (1, 2, 3):
-        send(PLB + 4 + o, out_b2.at[lax.rem(x + o, 4)], in_b2.at[o], x_mate(o))
     arrived(PLA + 2, in_a.at[2])
     arrived(PLA + 3, in_a.at[3])
     total = out_a[x] + in_a[2] + in_a[3]
     for n in range(4):
-        out_a2[n, 0:32, :] = total[32 * n : 32 * n + 32, :]
-        out_a2[n, 32:40, :] = total[128:136, :]
+        out_a2[n, 0:48, :] = total[48 * n : 48 * n + 48, :]
+        out_a2[n, 48:56, :] = total[192:200, :]
     for o in (1, 2, 3):
         send(PLA + 4 + o, out_a2.at[lax.rem(y + o, 4)], in_a2.at[o], y_mate(o))
     for q in (1, 3):
         cross_wait_rest(IMG, images, q, None)
     image_group(4, 6)
-    total_b = summed(PLB + 4, out_b2, x, in_b2)
-    total_a = summed(PLA + 4, out_a2, y, in_a2)
-    total = jnp.concatenate([total_a[:32, :], total_b], axis=0)
+    total = summed(PLA + 4, out_a2, y, in_a2)
     for j in range(8):
         tails[j, 0:6, :] = total[6 * j : 6 * j + 6, :]
-        tails[j, 6:8, :] = total_a[32:34, :]
+        tails[j, 6:8, :] = total[48:50, :]
     for j in range(8):
         @pl.when(first_owner + j != me)
         def _():
@@ -506,15 +493,11 @@
             pltpu.VMEM((768, 256), f32),
             pltpu.VMEM((768, 256), f32),
             pltpu.VMEM((8, 8, 256), f32),
-            pltpu.VMEM((4, 136, 256), f32),
-            pltpu.VMEM((4, 136, 256), f32),
-            pltpu.VMEM((136, 256), f32),
-            pltpu.VMEM((4, 64, 256), f32),
-            pltpu.VMEM((4, 64, 256), f32),
-            pltpu.VMEM((4, 40, 256), f32),
-            pltpu.VMEM((4, 40, 256), f32),
-            pltpu.VMEM((4, 16, 256), f32),
-            pltpu.VMEM((4, 16, 256), f32),
+            pltpu.VMEM((4, 200, 256), f32),
+            pltpu.VMEM((4, 200, 256), f32),
+            pltpu.VMEM((200, 256), f32),
+            pltpu.VMEM((4, 56, 256), f32),
+            pltpu.VMEM((4, 56, 256), f32),
             pltpu.SemaphoreType.DMA((16,)),
             pltpu.SemaphoreType.DMA((IDS,)),
             pltpu.SemaphoreType.DMA((IDS,)),

time: 71.7 us -> 72.7 us (1.014)
  Pallas kernels: 68.7 us -> 69.5 us
    pallas_call x1, Pallas kernels: 66.7 us -> 67.5 us  [shards(): pl.pallas_call(kernel, out_shape=(jax.ShapeDtypeStruct((8, 2 * B), f32),...]
where the time goes in v14:
time: 72.7 us; the launch traced here: 71.4 us
  Pallas kernels  69.5 us (96%)
  between operations  1.93 us (3%)
    pallas_call x1, Pallas kernels, shards(): pl.pallas_call(kernel, out_shape=(jax.ShapeDtypeStruct((8, 2 * B), f32),...  67.5 us
    pallas_call x1, Pallas kernels, shards(): pl.pallas_call(finish, out_shape=(jax.ShapeDtypeStruct((1,), f32), jax.Sh...  2.02 us

profile of v14, /device:TPU:1, one launch (start us, length us, event | category | flops | bytes accessed | tf_op | source)
XLA Modules:
  0.0 71.4 jit_solution(3331193745702005647)
XLA Ops:
  1.9 67.5 %contrastive.1 = (f32[8,256]{1,0:T(8,128)}, f32[6,1024]{1,0:T(8,128)}, f32[128,1024]{1,0:T(8,128)}, f32[128,128]{1,0:T(8,128)}) custom-call(f32[1]{0:T(128)S(6)} %copy.10.ls_ref, f32[1]{0:T(128)S(6)} %copy.11.lb_ref, bf16[128,1536]{1,0:T(8,128)(2,1)} %imgf_ref.1, bf16[128,4096]{1,0:T(8,128)(2,1)} %txtf_ref.1, bf16[1536,1024]{1,0:T(8,128)(2,1)} %imgh_ref.1, ...), custom_call_target="tpu_custom_call" | custom-call | flops 5000000000 | bytes 14000000 | tf_op jit(solution)/shard_map/contrastive/pallas_call | solution.py:459
  69.4 2.0 %finish.1 = (f32[1]{0:T(128)}, f32[2]{0:T(128)}, f32[6,1024]{1,0:T(8,128)}, f32[128,1024]{1,0:T(8,128)}) custom-call(f32[1]{0:T(128)S(6)} %copy.10.ls_ref, f32[8,256]{1,0:T(8,128)} %get-tuple-element.12.st_ref, f32[6,1024]{1,0:T(8,128)} %get-tuple-element.13.hgs_ref, f32[128,1024]{1,0:T(8,128)} %get-tuple-element.14.tgs_ref, ...), custom_call_target="tpu_custom_call" | custom-call | tf_op jit(solution)/shard_map/finish/pallas_call | solution.py:511

commit v15 on v10

--- a/solution.py
+++ b/solution.py
@@ -450,13 +450,27 @@
     drain(sent, sent_if)
 
 
-def finish(ls_ref, st_ref, hgs_ref, tgs_ref, tinv_ref, loss_ref, sg_ref, hg_ref, tg_ref):
+def finish(
+    ls_ref, st_ref, hgs_ref, tgs_ref, tinv_ref, loss_ref, sg_ref, hg_ref, tg_ref, block, load_sem, store_sem
+):
+    def span(n):
+        return pl.ds(n * 32, 32)
+
+    loads = [pltpu.make_async_copy(tgs_ref.at[span(n)], block.at[span(n)], load_sem.at[n]) for n in range(4)]
+    stores = [pltpu.make_async_copy(block.at[span(n)], tg_ref.at[span(n)], store_sem.at[n]) for n in range(4)]
+    for c in loads:
+        c.start()
+    for n in range(4):
+        loads[n].wait()
+        block[span(n), :] = block[span(n), :] * tinv_ref[span(n), 0:1]
+        stores[n].start()
     temper = jnp.exp(jnp.full((1, B), ls_ref[0], jnp.float32))
     loss_ref[0] = jnp.sum(st_ref[6:7, 0:B]) / PAIRS
     sg_ref[0] = jnp.sum(st_ref[6:7, B : 2 * B] * temper) / PAIRS
     sg_ref[1] = jnp.sum(st_ref[7:8, 0:B]) / PAIRS
     hg_ref[...] = hgs_ref[...] * (1.0 / B)
-    tg_ref[...] = tgs_ref[...] * tinv_ref[:, 0:1]
+    for c in stores:
+        c.wait()
 
 
 def shards(img_feats, txt_feats, img_head, txt_head, log_scale, logit_bias):
@@ -527,8 +541,13 @@
             jax.ShapeDtypeStruct((6, E), f32),
             jax.ShapeDtypeStruct((B, E), f32),
         ),
-        in_specs=[smem] + [vmem] * 4,
-        out_specs=(smem, smem, vmem, vmem),
+        in_specs=[smem, vmem, vmem, hbm, vmem],
+        out_specs=(smem, smem, vmem, hbm),
+        scratch_shapes=[
+            pltpu.VMEM((B, E), f32),
+            pltpu.SemaphoreType.DMA((4,)),
+            pltpu.SemaphoreType.DMA((4,)),
+        ],
         name="finish",
     )(log_scale, *sums)
     return loss.reshape(()), scalar_grads, head_grad, text_grad

time: 71.3 us -> 72.8 us (1.021)
  Pallas kernels: 68.8 us -> 70.2 us
    pallas_call x1, Pallas kernels: 2.02 us -> 3.47 us  [shards(): pl.pallas_call(finish, out_shape=(jax.ShapeDtypeStruct((1,), f32), jax.Sh...]
where the time goes in v15:
time: 72.8 us; the launch traced here: 72.2 us
  Pallas kernels  70.2 us (96%)
  between operations  1.93 us (3%)
    pallas_call x1, Pallas kernels, shards(): pl.pallas_call(kernel, out_shape=(jax.ShapeDtypeStruct((8, 2 * B), f32),...  66.8 us
    pallas_call x1, Pallas kernels, shards(): pl.pallas_call(finish, out_shape=(jax.ShapeDtypeStruct((1,), f32), jax.Sh...  3.47 us

profile of v15, /device:TPU:1, one launch (start us, length us, event | category | flops | bytes accessed | tf_op | source)
XLA Modules:
  0.0 72.2 jit_solution(16378164976337499307)
XLA Ops:
  1.9 66.8 %contrastive.1 = (f32[8,256]{1,0:T(8,128)}, f32[6,1024]{1,0:T(8,128)}, f32[128,1024]{1,0:T(8,128)}, f32[128,128]{1,0:T(8,128)}) custom-call(f32[1]{0:T(128)S(6)} %copy.10.ls_ref, f32[1]{0:T(128)S(6)} %copy.11.lb_ref, bf16[128,1536]{1,0:T(8,128)(2,1)} %imgf_ref.1, bf16[128,4096]{1,0:T(8,128)(2,1)} %txtf_ref.1, bf16[1536,1024]{1,0:T(8,128)(2,1)} %imgh_ref.1, ...), custom_call_target="tpu_custom_call" | custom-call | flops 5000000000 | bytes 14000000 | tf_op jit(solution)/shard_map/contrastive/pallas_call | solution.py:481
  68.7 3.5 %finish.1 = (f32[1]{0:T(128)}, f32[2]{0:T(128)}, f32[6,1024]{1,0:T(8,128)}, f32[128,1024]{1,0:T(8,128)}) custom-call(f32[1]{0:T(128)S(6)} %copy.10.ls_ref, f32[8,256]{1,0:T(8,128)} %get-tuple-element.12.st_ref, f32[6,1024]{1,0:T(8,128)} %get-tuple-element.13.hgs_ref, f32[128,1024]{1,0:T(8,128)} %get-tuple-element.14.tgs_ref, ...), custom_call_target="tpu_custom_call" | custom-call | tf_op jit(solution)/shard_map/finish/pallas_call | solution.py:536

commit v16 on v10

--- a/solution.py
+++ b/solution.py
@@ -338,12 +338,12 @@
     early, early_if = list(sent), list(sent_if)
     sent.clear()
     sent_if.clear()
+    own_wait(TXT, texts)
+    image_group(0)
     for q in (1, 3):
         row_wait(IMG, images, q, None)
         cross_send(IMG, images, q, None)
     opposite_send(IMG, images, None)
-    own_wait(TXT, texts)
-    image_group(0)
 
     for n in (1, 2, 3):
         arrived(DLO + n, window(n))
@@ -385,8 +385,8 @@
 
     row_wait(IMG, images, 2, None)
     cross_send(IMG, images, 2, None)
+    image_group(1, 3)
     hand_on(IMG, images, None)
-    image_group(1, 3)
     image_group(2)
     drain(early, early_if)
 

time: 71.3 us -> 71.7 us (level)
  no operation moved by 1% of the time
where the time goes in v16:
time: 71.7 us; the launch traced here: 71.3 us
  Pallas kernels  69.4 us (97%)
  between operations  1.93 us (3%)
    pallas_call x1, Pallas kernels, shards(): pl.pallas_call(kernel, out_shape=(jax.ShapeDtypeStruct((8, 2 * B), f32),...  67.4 us
    pallas_call x1, Pallas kernels, shards(): pl.pallas_call(finish, out_shape=(jax.ShapeDtypeStruct((1,), f32), jax.Sh...  2.02 us

profile of v16, /device:TPU:1, one launch (start us, length us, event | category | flops | bytes accessed | tf_op | source)
XLA Modules:
  0.0 71.3 jit_solution(3234662596772085367)
XLA Ops:
  1.9 67.4 %contrastive.1 = (f32[8,256]{1,0:T(8,128)}, f32[6,1024]{1,0:T(8,128)}, f32[128,1024]{1,0:T(8,128)}, f32[128,128]{1,0:T(8,128)}) custom-call(f32[1]{0:T(128)S(6)} %copy.10.ls_ref, f32[1]{0:T(128)S(6)} %copy.11.lb_ref, bf16[128,1536]{1,0:T(8,128)(2,1)} %imgf_ref.1, bf16[128,4096]{1,0:T(8,128)(2,1)} %txtf_ref.1, bf16[1536,1024]{1,0:T(8,128)(2,1)} %imgh_ref.1, ...), custom_call_target="tpu_custom_call" | custom-call | flops 5000000000 | bytes 14000000 | tf_op jit(solution)/shard_map/contrastive/pallas_call | solution.py:467
  69.3 2.0 %finish.1 = (f32[1]{0:T(128)}, f32[2]{0:T(128)}, f32[6,1024]{1,0:T(8,128)}, f32[128,1024]{1,0:T(8,128)}) custom-call(f32[1]{0:T(128)S(6)} %copy.10.ls_ref, f32[8,256]{1,0:T(8,128)} %get-tuple-element.12.st_ref, f32[6,1024]{1,0:T(8,128)} %get-tuple-element.13.hgs_ref, f32[128,1024]{1,0:T(8,128)} %get-tuple-element.14.tgs_ref, ...), custom_call_target="tpu_custom_call" | custom-call | tf_op jit(solution)/shard_map/finish/pallas_call | solution.py:522
